TPU v7x, 32 devices: a whole 2x2x4 slice. The times are simulated.
32 devices in a mesh: rep: 2 (over x), shard: 16 (over z, y, core).
Axes of the slice: x: 2, y: 2, z: 4, core: 2. Of those that a mesh axis runs over, the one named last changes fastest.
Arguments:
- tokens: bfloat16 [4096, 768], P(('rep', 'shard')), may hold values from -6 to 6
- cotangent: bfloat16 [4096, 768], P(('rep', 'shard')), may hold values from -6 to 6
- lengths: int32 [32, 3], P(('rep', 'shard')), may hold values from 1 to 96, 128 in all within a row
- routes: int32 [4096, 1], P(('rep', 'shard')), may hold values from 0 to 1; in each aligned block of 128 rows (0 to 127, 128 to 255, ...) at most 80 rows name the same one
- bucket_ids: int32 [255], replicated, may hold values from 0 to 31
- attn_in: bfloat16 [3, 768, 768], P(None, 'shard'), may hold values from -0.21875 to 0.21875
- attn_out: bfloat16 [768, 768], P('shard'), may hold values from -0.875 to 0.875
- gains: bfloat16 [2, 768], P(None, 'shard'), may hold values from 0.25 to 1.75
- router: bfloat16 [768, 2], P('shard'), may hold values from -0.109375 to 0.109375
- rel_table: bfloat16 [32, 12], P('shard'), may hold values from -4 to 4
- expert_in: bfloat16 [2, 768, 3072], P(None, 'shard'), may hold values from -0.21875 to 0.21875
- expert_out: bfloat16 [2, 3072, 768], P(None, 'shard'), may hold values from -0.21875 to 0.21875
Outputs:
- layer_out: bfloat16 [4096, 768], P(('rep', 'shard'))
- input_grad: float32 [4096, 768], P(('rep', 'shard'))
- grad_attn_in: float32 [3, 768, 768], P(None, 'shard')
- grad_attn_out: float32 [768, 768], P('shard')
- grad_gains: float32 [2, 768], P(None, 'shard')
- grad_router: float32 [768, 2], P('shard')
- grad_rel_table: float32 [32, 12], P('shard')
- grad_expert_in: float32 [2, 768, 3072], P(None, 'shard')
- grad_expert_out: float32 [2, 3072, 768], P(None, 'shard')
Inputs may be any that keep to these rules, and one draw needn't show every extreme that they name: Row b holds the lengths of the 3 sequences of device block b; they sum to 128, and some block has one of exactly 96. `routes`: within the 128 rows of one device no expert is named more than 80 times, and in every draw some device names some expert exactly 80 times.
All inputs are finite; a program needn't handle non-finite values.
Results may differ from a plain program's by a relative error of at most 0.012.
Values may be sent and summed in bfloat16 or wider, within the bound.
A program may use at most 192 MiB of HBM per device.

v0:
```python
import jax
import jax.numpy as jnp
from jax import lax
from jax.sharding import PartitionSpec as P

BUCKETS = 32
CAP = 80


epsilon = 1e-06


def rms_norm(values, gain):
    return values * lax.rsqrt(jnp.mean(values * values, axis=-1, keepdims=True) + epsilon) * gain


def gelu_tanh(values):
    return jax.nn.gelu(values, approximate=True)


def offsets_to_pairs(per_offset, length):
    heads = per_offset.shape[0]
    reverse = per_offset[:, ::-1]
    repeated = jnp.broadcast_to(reverse[:, None, :], (heads, length, 2 * length - 1))
    repeated = repeated.reshape(heads, length * (2 * length - 1))
    repeated = jnp.pad(repeated, ((0, 0), (0, length)))
    skewed = repeated.reshape(heads, length, 2 * length)[:, :, :length]
    return skewed[:, :, ::-1]


def pairs_to_offsets(grid, length):
    heads = grid.shape[0]
    flipped = grid[:, :, ::-1]
    padded = jnp.pad(flipped, ((0, 0), (0, 0), (0, length)))
    flat = padded.reshape(heads, 2 * length * length)[:, : length * (2 * length - 1)]
    skewed = flat.reshape(heads, length, 2 * length - 1)
    return jnp.sum(skewed, axis=1)[:, ::-1]


def shards(
    tokens,
    cotangent,
    lengths,
    routes,
    bucket_ids,
    attn_in,
    attn_out,
    gains,
    router,
    rel_table,
    expert_in,
    expert_out,
):
    highest = lax.Precision.HIGHEST
    length = tokens.shape[0]
    width = tokens.shape[1]
    heads = rel_table.shape[1]
    head_size = width // heads
    experts = expert_in.shape[0]
    capacity = CAP
    bucket_count = BUCKETS
    full_in, full_out, full_gains, full_router, full_table = (
        lax.all_gather(attn_in, "shard", axis=1, tiled=True),
        lax.all_gather(attn_out, "shard", axis=0, tiled=True),
        lax.all_gather(gains, "shard", axis=1, tiled=True),
        lax.all_gather(router, "shard", axis=0, tiled=True),
        lax.all_gather(rel_table, "shard", axis=0, tiled=True),
    )
    inputs = tokens.astype(jnp.float32)
    gain_attn = full_gains[0].astype(jnp.float32)
    gain_ffn = full_gains[1].astype(jnp.float32)
    normed = rms_norm(inputs, gain_attn).astype(jnp.bfloat16)
    projected = jnp.einsum(
        "td,kde->kte", normed, full_in, preferred_element_type=jnp.float32
    ).astype(jnp.bfloat16)
    query = projected[0].reshape(length, heads, head_size)
    keys = projected[1].reshape(length, heads, head_size)
    values = projected[2].reshape(length, heads, head_size)
    places = jnp.arange(length, dtype=jnp.int32)
    offset_onehot = (
        bucket_ids[:, None] == jnp.arange(bucket_count, dtype=jnp.int32)[None, :]
    ).astype(jnp.float32)
    offset_bias = jnp.einsum(
        "ob,bh->ho", offset_onehot, full_table.astype(jnp.float32), precision=highest
    )
    bias = offsets_to_pairs(offset_bias, length)
    ends = jnp.cumsum(lengths[0])
    segment = jnp.sum((places[:, None] >= ends[None, :]).astype(jnp.int32), axis=1)
    allowed = segment[:, None] == segment[None, :]

    def masked_scores():
        raw = jnp.einsum("qhc,khc->hqk", query, keys, preferred_element_type=jnp.float32) * 0.125
        return jnp.where(allowed[None], raw + bias, -1e30)

    scores = masked_scores()
    peak = jnp.max(scores, axis=-1, keepdims=True)
    expo = jnp.exp(scores - peak)
    totals = jnp.sum(expo, axis=-1, keepdims=True)
    logsum = peak + jnp.log(totals)
    probs_low = (expo / totals).astype(jnp.bfloat16)
    context = jnp.einsum("hqk,khc->qhc", probs_low, values, preferred_element_type=jnp.float32)
    context = context.astype(jnp.bfloat16).reshape(length, width)
    hidden = inputs + jnp.dot(context, full_out, preferred_element_type=jnp.float32)
    normed_ffn = rms_norm(hidden, gain_ffn).astype(jnp.bfloat16)
    logits = jnp.dot(normed_ffn, full_router, preferred_element_type=jnp.float32)
    gate_probs = jax.nn.softmax(logits, axis=-1)
    chosen = routes[:, 0]
    picked = chosen[:, None] == jnp.arange(experts, dtype=jnp.int32)[None, :]
    gate = jnp.sum(jnp.where(picked, gate_probs, 0.0), axis=1)
    ranks = jnp.cumsum(picked.astype(jnp.int32), axis=0) - 1
    slot = chosen * capacity + jnp.sum(jnp.where(picked, ranks, 0), axis=1)
    dispatch = (jnp.arange(experts * capacity, dtype=jnp.int32)[:, None] == slot[None, :]).astype(
        jnp.bfloat16
    )
    buffers = jnp.dot(dispatch, normed_ffn, preferred_element_type=jnp.float32).astype(jnp.bfloat16)
    buffers = buffers.reshape(experts, capacity, width)
    before_list = []
    active_list = []
    returned_list = []
    for expert in range(experts):
        batch = buffers[expert]
        whole_in = lax.all_gather(expert_in[expert], "shard", axis=0, tiled=True)
        before = jnp.dot(batch, whole_in, preferred_element_type=jnp.float32)
        active = gelu_tanh(before).astype(jnp.bfloat16)
        whole_out = lax.all_gather(expert_out[expert], "shard", axis=0, tiled=True)
        returned = jnp.dot(active, whole_out, preferred_element_type=jnp.float32)
        before_list.append(before)
        active_list.append(active)
        returned_list.append(returned)
    returned_all = jnp.concatenate(returned_list, axis=0)
    gathered = jnp.take(returned_all, slot, axis=0)
    layer_out = (hidden + gate[:, None] * gathered).astype(jnp.bfloat16)
    upstream = cotangent.astype(jnp.float32)
    gate_grad = jnp.sum(upstream * gathered, axis=1)
    scaled = (gate[:, None] * upstream).astype(jnp.bfloat16)
    returned_grad = jnp.dot(dispatch, scaled, preferred_element_type=jnp.float32).astype(
        jnp.bfloat16
    )
    returned_grad = returned_grad.reshape(experts, capacity, width)
    batch_grads = []
    inner_shards = []
    outer_shards = []
    for expert in range(experts):
        batch = buffers[expert]
        active = active_list[expert]
        out_grad = returned_grad[expert]
        out_matrix = lax.all_gather(expert_out[expert], "shard", axis=0, tiled=True)
        active_grad = jnp.einsum(
            "cd,fd->cf", out_grad, out_matrix, preferred_element_type=jnp.float32
        )
        before_grad = jax.vjp(gelu_tanh, before_list[expert])[1](active_grad)[0].astype(
            jnp.bfloat16
        )
        in_matrix = lax.all_gather(expert_in[expert], "shard", axis=0, tiled=True)
        batch_grad = jnp.einsum(
            "cf,df->cd", before_grad, in_matrix, preferred_element_type=jnp.float32
        )
        batch_grads.append(batch_grad)
        inner_shard = lax.psum_scatter(
            jnp.einsum("cd,cf->df", batch, before_grad, preferred_element_type=jnp.float32),
            "shard",
            scatter_dimension=0,
            tiled=True,
        )
        outer_shard = lax.psum_scatter(
            jnp.einsum("cf,cd->fd", active, out_grad, preferred_element_type=jnp.float32),
            "shard",
            scatter_dimension=0,
            tiled=True,
        )
        inner_shards.append(inner_shard)
        outer_shards.append(outer_shard)
    batch_all = jnp.concatenate(batch_grads, axis=0)
    ffn_normed_grad = jnp.take(batch_all, slot, axis=0)
    prob_grad = jnp.where(picked, gate_grad[:, None], 0.0)
    logit_grad = gate_probs * (prob_grad - jnp.sum(gate_probs * prob_grad, axis=1, keepdims=True))
    normed_wide = normed_ffn.astype(jnp.float32)
    router_grad = jnp.einsum("td,te->de", normed_wide, logit_grad, precision=highest)
    ffn_normed_grad = ffn_normed_grad + jnp.einsum(
        "te,de->td", logit_grad, full_router.astype(jnp.float32), precision=highest
    )
    norm_pull = jax.vjp(rms_norm, hidden, gain_ffn)[1]
    hidden_from_norm, gain_ffn_grad = norm_pull(ffn_normed_grad)
    hidden_grad = upstream + hidden_from_norm
    attn_grad = hidden_grad.astype(jnp.bfloat16)
    attn_out_grad = jnp.einsum("td,te->de", context, attn_grad, preferred_element_type=jnp.float32)
    context_grad = jnp.einsum("te,de->td", attn_grad, full_out, preferred_element_type=jnp.float32)
    context_grad = context_grad.astype(jnp.bfloat16).reshape(length, heads, head_size)
    probs = jnp.exp(masked_scores() - logsum)
    probs_back = probs.astype(jnp.bfloat16)
    prob_grad_attn = jnp.einsum(
        "qhc,khc->hqk", context_grad, values, preferred_element_type=jnp.float32
    )
    value_grad = jnp.einsum(
        "hqk,qhc->khc", probs_back, context_grad, preferred_element_type=jnp.float32
    )
    score_grad = probs * (prob_grad_attn - jnp.sum(probs * prob_grad_attn, axis=-1, keepdims=True))
    offset_grad = pairs_to_offsets(score_grad, length)
    table_grad = jnp.einsum("ho,ob->bh", offset_grad, offset_onehot, precision=highest)
    score_low = score_grad.astype(jnp.bfloat16)
    query_grad = (
        jnp.einsum("hqk,khc->qhc", score_low, keys, preferred_element_type=jnp.float32) * 0.125
    )
    key_grad = (
        jnp.einsum("hqk,qhc->khc", score_low, query, preferred_element_type=jnp.float32) * 0.125
    )
    projected_grad = jnp.stack(
        [
            query_grad.reshape(length, width),
            key_grad.reshape(length, width),
            value_grad.reshape(length, width),
        ]
    ).astype(jnp.bfloat16)
    attn_in_grad = jnp.einsum(
        "td,kte->kde", normed, projected_grad, preferred_element_type=jnp.float32
    )
    normed_grad = jnp.einsum(
        "kte,kde->td", projected_grad, full_in, preferred_element_type=jnp.float32
    )
    input_pull = jax.vjp(rms_norm, inputs, gain_attn)[1]
    input_from_norm, gain_attn_grad = input_pull(normed_grad)
    input_grad = hidden_grad + input_from_norm
    gains_grad = jnp.stack([gain_attn_grad, gain_ffn_grad])
    in_shard, out_shard, gains_shard, router_shard, table_shard = (
        lax.psum_scatter(attn_in_grad, "shard", scatter_dimension=1, tiled=True),
        lax.psum_scatter(attn_out_grad, "shard", scatter_dimension=0, tiled=True),
        lax.psum_scatter(gains_grad, "shard", scatter_dimension=1, tiled=True),
        lax.psum_scatter(router_grad, "shard", scatter_dimension=0, tiled=True),
        lax.psum_scatter(table_grad, "shard", scatter_dimension=0, tiled=True),
    )
    expert_in_grad = jnp.stack(inner_shards)
    expert_out_grad = jnp.stack(outer_shards)
    in_shard, out_shard, gains_shard, router_shard, table_shard, expert_in_grad, expert_out_grad = (
        lax.psum(
            (
                in_shard,
                out_shard,
                gains_shard,
                router_shard,
                table_shard,
                expert_in_grad,
                expert_out_grad,
            ),
            "rep",
        )
    )
    return (
        layer_out,
        input_grad,
        in_shard,
        out_shard,
        gains_shard,
        router_shard,
        table_shard,
        expert_in_grad,
        expert_out_grad,
    )


def solution(mesh):
    placed = (
        P(("rep", "shard"), None),
        P(("rep", "shard"), None),
        P(("rep", "shard"), None),
        P(("rep", "shard"), None),
        P(),
        P(None, "shard", None),
        P("shard", None),
        P(None, "shard"),
        P("shard", None),
        P("shard", None),
        P(None, "shard", None),
        P(None, "shard", None),
    )
    return jax.shard_map(
        shards,
        mesh=mesh,
        in_specs=placed,
        out_specs=(
            P(("rep", "shard"), None),
            P(("rep", "shard"), None),
            P(None, "shard", None),
            P("shard", None),
            P(None, "shard"),
            P("shard", None),
            P("shard", None),
            P(None, "shard", None),
            P(None, "shard", None),
        ),
        check_vma=False,
    )
```

profile of v0, /device:TPU:0, one launch (start us, length us, event | category | flops | bytes accessed | tf_op | source)
XLA Modules:
  0.0 1300.3 jit_solution(768440275594427823)
XLA Ops:
  13.8 23.2 %all-gather.4 = bf16[16,48,2]{1,2,0:T(2,128)(2,1)S(1)} all-gather(bf16[1,48,2]{1,2,0:T(2,128)(2,1)} %bitcast.144), channel_id=1, replica_groups=mesh['rep'=2,'shard'=16] {'shard'}, dimensions={0}, use_global_device_ids=true | all-gather | bytes 3264 | tf_op jit(solution)/shard_map/all_gather | solution.py:65
  37.1 17.5 %all-gather.6 = bf16[16,48,2]{1,2,0:T(2,128)(2,1)S(1)} all-gather(bf16[1,48,2]{1,2,0:T(2,128)(2,1)} %bitcast.145), channel_id=1, replica_groups=mesh['rep'=2,'shard'=16] {'shard'}, dimensions={0}, use_global_device_ids=true | all-gather | bytes 3264 | tf_op jit(solution)/shard_map/all_gather | solution.py:66
  54.7 18.9 %all-gather.5 = bf16[16,2,12]{2,1,0:T(2,128)(2,1)S(1)} all-gather(bf16[1,2,12]{2,1,0:T(2,128)(2,1)} %bitcast.146), channel_id=1, replica_groups=mesh['rep'=2,'shard'=16] {'shard'}, dimensions={0}, use_global_device_ids=true | all-gather | bytes 816 | tf_op jit(solution)/shard_map/all_gather | solution.py:67
  86.5 13.4 %all-gather.16.cloned.1.call-done = bf16[768,768]{1,0:T(8,128)(2,1)} async-done(((bf16[48,768]{1,0:T(8,128)(2,1)}), bf16[768,768]{1,0:T(8,128)(2,1)}) %all-gather.16.cloned.1.call-update) | async-done | bytes 1179664 | tf_op jit(solution)/shard_map/all_gather | solution.py:64
  103.0 51.6 %all-gather.22.cloned.1.call-done = bf16[1,768,3072]{2,1,0:T(8,128)(2,1)} async-done(((bf16[1,48,3072]{2,1,0:T(8,128)(2,1)}), bf16[1,768,3072]{2,1,0:T(8,128)(2,1)}) %all-gather.22.cloned.1.call-update) | async-done | bytes 4718608 | tf_op jit(solution)/shard_map/all_gather | solution.py:122
  157.9 51.4 %all-gather.18.cloned.1.call-done = bf16[1,768,3072]{2,1,0:T(8,128)(2,1)} async-done(((bf16[1,48,3072]{2,1,0:T(8,128)(2,1)}), bf16[1,768,3072]{2,1,0:T(8,128)(2,1)}) %all-gather.18.cloned.1.call-update) | async-done | bytes 4718608 | tf_op jit(solution)/shard_map/all_gather | solution.py:122
  212.6 51.4 %all-gather.24.cloned.1.call-done = bf16[1,3072,768]{2,1,0:T(8,128)(2,1)} async-done(((bf16[1,192,768]{2,1,0:T(8,128)(2,1)}), bf16[1,3072,768]{2,1,0:T(8,128)(2,1)}) %all-gather.24.cloned.1.call-update) | async-done | bytes 4718608 | tf_op jit(solution)/shard_map/all_gather | solution.py:125
  268.0 50.7 %all-gather.20.cloned.1.call-done = bf16[1,3072,768]{2,1,0:T(8,128)(2,1)} async-done(((bf16[1,192,768]{2,1,0:T(8,128)(2,1)}), bf16[1,3072,768]{2,1,0:T(8,128)(2,1)}) %all-gather.20.cloned.1.call-update) | async-done | bytes 4718608 | tf_op jit(solution)/shard_map/all_gather | solution.py:125
  326.5 4.1 fusion.34
  357.0 11.0 copy.96
  369.2 5.7 fusion.67
  375.9 5.1 fusion.64
  381.9 5.1 fusion.61
  387.1 5.0 fusion.58
  402.0 149.6 %all-reduce.9.cloned.1.call-done = f32[3,768,768]{2,0,1:T(4,128)} async-done(((f32[3,768,768]{2,0,1:T(4,128)}), f32[3,768,768]{2,0,1:T(4,128)}) %all-reduce.9.cloned.1.call-update) | async-done | bytes 7077904
  553.6 114.1 %reduce-scatter.14.cloned.1.call-done = f32[48,3072]{1,0:T(8,128)} async-done(((f32[768,3072]{1,0:T(8,128)}), f32[48,3072]{1,0:T(8,128)}) %reduce-scatter.14.cloned.1.call-update) | async-done | bytes 589840 | tf_op jit(solution)/shard_map/reduce_scatter | solution.py:159
  667.6 115.2 %reduce-scatter.16.cloned.1.call-done = f32[48,3072]{1,0:T(8,128)} async-done(((f32[768,3072]{1,0:T(8,128)}), f32[48,3072]{1,0:T(8,128)}) %reduce-scatter.16.cloned.1.call-update) | async-done | bytes 589840 | tf_op jit(solution)/shard_map/reduce_scatter | solution.py:159
  785.2 113.3 %reduce-scatter.18.cloned.1.call-done = f32[192,768]{1,0:T(8,128)} async-done(((f32[3072,768]{1,0:T(8,128)}), f32[192,768]{1,0:T(8,128)}) %reduce-scatter.18.cloned.1.call-update) | async-done | bytes 589840 | tf_op jit(solution)/shard_map/reduce_scatter | solution.py:165
  898.6 115.2 %reduce-scatter.20.cloned.1.call-done = f32[192,768]{1,0:T(8,128)} async-done(((f32[3072,768]{1,0:T(8,128)}), f32[192,768]{1,0:T(8,128)}) %reduce-scatter.20.cloned.1.call-update) | async-done | bytes 589840 | tf_op jit(solution)/shard_map/reduce_scatter | solution.py:165
  1016.1 64.5 %reduce-scatter.12.cloned.1.call-done = f32[48,768]{1,0:T(8,128)} async-done(((f32[768,768]{1,0:T(8,128)}), f32[48,768]{1,0:T(8,128)}) %reduce-scatter.12.cloned.1.call-update) | async-done | bytes 147472 | tf_op jit(solution)/shard_map/reduce_scatter | solution.py:226
  1089.3 57.6 %all-reduce.3 = f32[32,12]{1,0:T(8,128)S(1)} all-reduce(f32[32,12]{1,0:T(8,128)S(1)} %fusion.75), channel_id=10, replica_groups=mesh['rep'=2,'shard'=16] {'shard'}, use_global_device_ids=true, to_apply=%region_27.29.clone | all-reduce | flops 384 | bytes 3072
  1148.7 49.0 %reduce-scatter.24.cloned.1.call-done = f32[48,2]{1,0:T(8,128)} async-done(((f32[768,2]{1,0:T(8,128)}), f32[48,2]{1,0:T(8,128)}) %reduce-scatter.24.cloned.1.call-update) | async-done | bytes 400
  1198.5 5.5 all-reduce.4
  1204.0 81.5 %all-reduce.11.cloned.1.call-done = (f32[3,48,768]{2,0,1:T(4,128)}, f32[48,768]{1,0:T(8,128)}, f32[2,48,3072]{2,1,0:T(8,128)}, f32[2,192,768]{2,1,0:T(8,128)}) async-done(((f32[3,48,768]{2,0,1:T(4,128)}, f32[48,768]{1,0:T(8,128)}, f32[2,48,3072]{2,1,0:T(8,128)}, f32[2,192,768]{2,1,0:T(8,128)}), (f32[3,48,768]{2,0,1:T(4,128)}, f32[48,768]{1,0:T(8,128)}, f32[2,48,3072]{2,1,0:T(8,128)}, ...) | async-done | bytes 2949136 | tf_op jit(solution)/shard_map/psum | solution.py:234
  (205 shorter events, 104.5 us)
Async XLA Ops:
  7.2 75.3 %all-gather.14.cloned.1.call-start = ((), (), s32[]{:S(2)}) async-start(), calls=%async_computation.7 | async-start | bytes 3760128 | tf_op jit(solution)/shard_map/all_gather | solution.py:63
  7.9 92.0 %all-gather.16.cloned.1.call-start = ((), (), s32[]{:S(2)}) async-start(), calls=%async_computation.8 | async-start | bytes 1253376 | tf_op jit(solution)/shard_map/all_gather | solution.py:64
  8.7 146.0 %all-gather.22.cloned.1.call-start = ((), (), s32[]{:S(2)}) async-start(), calls=%async_computation.16 | async-start | bytes 5013504 | tf_op jit(solution)/shard_map/all_gather | solution.py:122
  10.6 198.7 %all-gather.18.cloned.1.call-start = ((), (), s32[]{:S(2)}) async-start(), calls=%async_computation.14 | async-start | bytes 5013504 | tf_op jit(solution)/shard_map/all_gather | solution.py:122
  11.2 252.8 %all-gather.24.cloned.1.call-start = ((), (), s32[]{:S(2)}) async-start(), calls=%async_computation.17 | async-start | bytes 5013504 | tf_op jit(solution)/shard_map/all_gather | solution.py:125
  13.2 305.5 %all-gather.20.cloned.1.call-start = ((), (), s32[]{:S(2)}) async-start(), calls=%async_computation.15 | async-start | bytes 5013504 | tf_op jit(solution)/shard_map/all_gather | solution.py:125
  13.8 537.8 %all-reduce.9.cloned.1.call-start = ((), (), s32[]{:S(2)}) async-start(), calls=%async_computation.20 | async-start | bytes 18874368
  85.4 16.3 %copy-start.13 = (bf16[1,128,768]{1,2,0:T(8,128)(2,1)}, bf16[1,128,768]{1,2,0:T(8,128)(2,1)S(1)}, u32[]{:S(2)}) copy-start(bf16[1,128,768]{1,2,0:T(8,128)(2,1)S(1)} %copy.82) | copy-start | bytes 589828
  85.6 17.2 %copy-start.14 = (bf16[1,128,768]{1,2,0:T(8,128)(2,1)}, bf16[1,128,768]{1,2,0:T(8,128)(2,1)S(1)}, u32[]{:S(2)}) copy-start(bf16[1,128,768]{1,2,0:T(8,128)(2,1)S(1)} %copy.81) | copy-start | bytes 589828
  85.7 72.2 %copy-start.20 = (bf16[1,128,768]{1,2,0:T(8,128)(2,1)}, bf16[1,128,768]{1,2,0:T(8,128)(2,1)S(1)}, u32[]{:S(2)}) copy-start(bf16[1,128,768]{1,2,0:T(8,128)(2,1)S(1)} %copy.80) | copy-start | bytes 589828
  86.5 16.5 %copy-start.18 = (bf16[12,64,128]{2,1,0:T(8,128)(2,1)}, bf16[12,64,128]{2,1,0:T(8,128)(2,1)S(1)}, u32[]{:S(2)}) copy-start(bf16[12,64,128]{2,1,0:T(8,128)(2,1)S(1)} %convolution_convert_fusion.5) | copy-start | bytes 589828
  102.5 110.1 %copy-start.5 = (bf16[128,768]{1,0:T(8,128)(2,1)}, bf16[128,768]{1,0:T(8,128)(2,1)S(1)}, u32[]{:S(2)}) copy-start(bf16[128,768]{1,0:T(8,128)(2,1)S(1)} %multiply_convert_fusion.2) | copy-start | bytes 589828
  103.0 109.6 %copy-start.7 = (bf16[160,768]{1,0:T(8,128)(2,1)}, bf16[160,768]{1,0:T(8,128)(2,1)S(1)}, u32[]{:S(2)}) copy-start(bf16[160,768]{1,0:T(8,128)(2,1)S(1)} %convolution_convert_fusion.2) | copy-start | bytes 737284
  323.7 7.0 copy-start.4
  326.5 7.4 slice-start.2
  368.1 299.6 %reduce-scatter.14.cloned.1.call-start = ((), (), s32[]{:S(2)}) async-start(), calls=%async_computation.10 | async-start | bytes 10027008 | tf_op jit(solution)/shard_map/reduce_scatter | solution.py:159
  374.9 408.0 %reduce-scatter.16.cloned.1.call-start = ((), (), s32[]{:S(2)}) async-start(), calls=%async_computation.11 | async-start | bytes 10027008 | tf_op jit(solution)/shard_map/reduce_scatter | solution.py:159
  381.0 517.5 %reduce-scatter.18.cloned.1.call-start = ((), (), s32[]{:S(2)}) async-start(), calls=%async_computation.12 | async-start | bytes 10027008 | tf_op jit(solution)/shard_map/reduce_scatter | solution.py:165
  387.0 626.8 %reduce-scatter.20.cloned.1.call-start = ((), (), s32[]{:S(2)}) async-start(), calls=%async_computation.13 | async-start | bytes 10027008 | tf_op jit(solution)/shard_map/reduce_scatter | solution.py:165
  392.1 688.5 %reduce-scatter.12.cloned.1.call-start = ((), (), s32[]{:S(2)}) async-start(), calls=%async_computation.9 | async-start | bytes 2506752 | tf_op jit(solution)/shard_map/reduce_scatter | solution.py:226
  394.8 753.0 %reduce-scatter.22.cloned.1.call-start = ((), (), s32[]{:S(2)}) async-start(), calls=%async_computation.18 | async-start | bytes 417792
  400.7 797.0 %reduce-scatter.24.cloned.1.call-start = ((), (), s32[]{:S(2)}) async-start(), calls=%async_computation.19 | async-start | bytes 417792
  401.9 679.4 %copy-start.1 = (f32[12,128,128]{1,2,0:T(8,128)S(1)}, f32[12,128,128]{1,2,0:T(8,128)}, u32[]{:S(2)}) copy-start(f32[12,128,128]{1,2,0:T(8,128)} %copy-done) | copy-start | bytes 2359300
  401.9 883.6 %all-reduce.11.cloned.1.call-start = ((), (), s32[]{:S(2)}) async-start(), calls=%async_computation.21 | async-start | bytes 6193152 | tf_op jit(solution)/shard_map/psum | solution.py:234
  (25 other events, 75.7 us)
Sparse Core Ops, SparseCore 0:
  10.3 49.9 all-gather.13
  62.6 37.3 all-gather.15
  102.2 52.3 all-gather.21
  157.3 51.9 all-gather.17
  212.0 51.9 all-gather.23
  266.7 51.9 all-gather.19
  368.2 183.3 all-reduce.8
  556.2 111.3 reduce-scatter.13
  671.8 111.0 reduce-scatter.15
  787.4 111.1 reduce-scatter.17
  902.7 111.0 reduce-scatter.19
  1017.9 62.7 reduce-scatter.11
  1084.7 54.5 reduce-scatter.21
  1143.1 54.5 reduce-scatter.23
  1201.2 84.2 all-reduce.10
where the time goes:
time: 1300 us
  waiting for transfers between devices  1020 us (78%)
  blocking collectives  123 us (9%)
  matrix products  72.4 us (6%)
  local copies, waits for them, and re-layouts  51.6 us (4%)
  between operations  16 us (1%)
  other arithmetic  13.3 us (1%)
    reduce_scatter x2, waiting for transfers between devices, shards(): lax.psum_scatter(jnp.einsum('cd,cf->df', batch, before_grad, preferred_el...  229 us
    reduce_scatter x2, waiting for transfers between devices, shards(): lax.psum_scatter(jnp.einsum('cf,cd->fd', active, out_grad, preferred_elem...  229 us
    unnamed x18, waiting for transfers between devices  201 us
    all_gather x2, waiting for transfers between devices, shards(): whole_in = lax.all_gather(expert_in[expert], 'shard', axis=0, tiled=True)  103 us
    all_gather x2, waiting for transfers between devices, shards(): whole_out = lax.all_gather(expert_out[expert], 'shard', axis=0, tiled=True)  102 us
    psum x1, waiting for transfers between devices, shards(): lax.psum((in_shard, out_shard, gains_shard, router_shard, table_shard, ex...  81.5 us
    reduce_scatter x1, waiting for transfers between devices, shards(): lax.psum_scatter(attn_out_grad, 'shard', scatter_dimension=0, tiled=True)  64.5 us
    unnamed x1, blocking collectives  57.6 us
  transfers between devices with their start and end apart: 15, of which 13 were waited for; matrix products, arithmetic and copies ran while one was open for 6% of the time, Pallas kernels for 0%

commit v1 on v0

v1 whole, which is shorter than its diff:
```python
import functools

import jax
import jax.numpy as jnp
from jax import lax
from jax.sharding import PartitionSpec as P

BUCKETS = 32
CAP = 80


epsilon = 1e-06


def rms_norm(values, gain):
    return values * lax.rsqrt(jnp.mean(values * values, axis=-1, keepdims=True) + epsilon) * gain


def gelu_tanh(values):
    return jax.nn.gelu(values, approximate=True)


def offsets_to_pairs(per_offset, length):
    heads = per_offset.shape[0]
    reverse = per_offset[:, ::-1]
    repeated = jnp.broadcast_to(reverse[:, None, :], (heads, length, 2 * length - 1))
    repeated = repeated.reshape(heads, length * (2 * length - 1))
    repeated = jnp.pad(repeated, ((0, 0), (0, length)))
    skewed = repeated.reshape(heads, length, 2 * length)[:, :, :length]
    return skewed[:, :, ::-1]


def pairs_to_offsets(grid, length):
    heads = grid.shape[0]
    flipped = grid[:, :, ::-1]
    padded = jnp.pad(flipped, ((0, 0), (0, 0), (0, length)))
    flat = padded.reshape(heads, 2 * length * length)[:, : length * (2 * length - 1)]
    skewed = flat.reshape(heads, length, 2 * length - 1)
    return jnp.sum(skewed, axis=1)[:, ::-1]


def swap(array, size):
    return lax.ppermute(array, "shard", [(i, i ^ 1) for i in range(size)])


def pair_order(core, mine, other, axis):
    first = jnp.where(core == 0, mine, other)
    second = jnp.where(core == 0, other, mine)
    return jnp.concatenate([first, second], axis=axis)


def rep_sum(array, reps):
    if reps == 2:
        other = lax.ppermute(array, "rep", [(0, 1), (1, 0)])
        return array.astype(jnp.float32) + other.astype(jnp.float32)
    return lax.psum(array.astype(jnp.float32), "rep")


def pick(array, index, axis=0):
    return lax.dynamic_index_in_dim(array, index, axis, keepdims=False)


def pad_row(values, width):
    flat = values.reshape(-1)
    return jnp.pad(flat, (0, width - flat.shape[0])).reshape(1, width)


def shards(
    size,
    reps,
    tokens,
    cotangent,
    lengths,
    routes,
    bucket_ids,
    attn_in,
    attn_out,
    gains,
    router,
    rel_table,
    expert_in,
    expert_out,
):
    highest = lax.Precision.HIGHEST
    low = jnp.bfloat16
    length, width = tokens.shape
    heads = rel_table.shape[1]
    head_size = width // heads
    experts = expert_in.shape[0]
    capacity = CAP
    bucket_count = BUCKETS
    chips = size // 2
    rows = width // size
    hidden_units = expert_in.shape[2]
    strip = hidden_units // chips
    groups = [[2 * j + c for j in range(chips)] for c in range(2)]
    core = lax.axis_index("shard") % 2

    packed = jnp.concatenate(
        [
            attn_in.reshape(3 * rows, width),
            attn_out,
            pad_row(gains, width),
            pad_row(router, width),
            pad_row(rel_table, width),
        ],
        axis=0,
    )
    depth = packed.shape[0]
    extra = -depth % 16
    packed = jnp.pad(packed, ((0, extra), (0, 0)))
    depth = depth + extra
    same = lax.all_gather(packed, "shard", axis=0, tiled=False, axis_index_groups=groups)
    other = swap(same, size)
    whole = jnp.stack(
        [jnp.where(core == 0, same, other), jnp.where(core == 0, other, same)], axis=1
    ).reshape(size, depth, width)
    full_in = whole[:, : 3 * rows].reshape(size, 3, rows, width)
    full_in = jnp.transpose(full_in, (1, 0, 2, 3)).reshape(3, width, width)
    full_out = whole[:, 3 * rows : 4 * rows].reshape(width, width)
    spot = 4 * rows
    full_gains = whole[:, spot, : 2 * rows].reshape(size, 2, rows)
    full_gains = jnp.transpose(full_gains, (1, 0, 2)).reshape(2, width)
    full_router = whole[:, spot + 1, : experts * rows].reshape(width, experts)
    table_rows = bucket_count // size
    full_table = whole[:, spot + 2, : table_rows * heads].reshape(bucket_count, heads)

    in_mine = pick(expert_in, core)
    in_other = swap(pick(expert_in, 1 - core), size)
    in_rows = pair_order(core, in_mine, in_other, 0).reshape(2 * rows, chips, strip)
    in_rows = jnp.transpose(in_rows, (1, 0, 2))
    in_strip = lax.all_to_all(
        in_rows, "shard", 0, 0, axis_index_groups=groups, tiled=True
    ).reshape(width, strip)
    out_mine = pick(expert_out, core)
    out_other = swap(pick(expert_out, 1 - core), size)
    out_strip = pair_order(core, out_mine, out_other, 0)

    inputs = tokens.astype(jnp.float32)
    upstream = cotangent.astype(jnp.float32)
    gain_attn = full_gains[0].astype(jnp.float32)
    gain_ffn = full_gains[1].astype(jnp.float32)
    normed = rms_norm(inputs, gain_attn).astype(low)
    projected = jnp.einsum(
        "td,kde->kte", normed, full_in, preferred_element_type=jnp.float32
    ).astype(low)
    query = projected[0].reshape(length, heads, head_size)
    keys = projected[1].reshape(length, heads, head_size)
    values = projected[2].reshape(length, heads, head_size)
    places = jnp.arange(length, dtype=jnp.int32)
    offset_onehot = (
        bucket_ids[:, None] == jnp.arange(bucket_count, dtype=jnp.int32)[None, :]
    ).astype(jnp.float32)
    offset_bias = jnp.einsum(
        "ob,bh->ho", offset_onehot, full_table.astype(jnp.float32), precision=highest
    )
    bias = offsets_to_pairs(offset_bias, length)
    seqs = jnp.arange(lengths.shape[1], dtype=jnp.int32)
    ends = jnp.sum(jnp.where(seqs[None, :] <= seqs[:, None], lengths[0][None, :], 0), axis=1)
    segment = jnp.sum((places[:, None] >= ends[None, :]).astype(jnp.int32), axis=1)
    allowed = segment[:, None] == segment[None, :]
    raw = jnp.einsum("qhc,khc->hqk", query, keys, preferred_element_type=jnp.float32) * 0.125
    scores = jnp.where(allowed[None], raw + bias, -1e30)
    peak = jnp.max(scores, axis=-1, keepdims=True)
    expo = jnp.exp(scores - peak)
    totals = jnp.sum(expo, axis=-1, keepdims=True)
    probs = expo / totals
    probs_low = probs.astype(low)
    context = jnp.einsum("hqk,khc->qhc", probs_low, values, preferred_element_type=jnp.float32)
    context = context.astype(low).reshape(length, width)
    hidden = inputs + jnp.dot(context, full_out, preferred_element_type=jnp.float32)
    normed_ffn = rms_norm(hidden, gain_ffn).astype(low)
    logits = jnp.dot(normed_ffn, full_router, preferred_element_type=jnp.float32)
    gate_probs = jax.nn.softmax(logits, axis=-1)
    chosen = routes[:, 0]
    picked = chosen[:, None] == jnp.arange(experts, dtype=jnp.int32)[None, :]
    gate = jnp.sum(jnp.where(picked, gate_probs, 0.0), axis=1)
    earlier = (places[None, :] < places[:, None]).astype(low)
    ranks = jnp.dot(earlier, picked.astype(low), preferred_element_type=jnp.float32)
    rank = jnp.sum(jnp.where(picked, ranks, 0.0), axis=1).astype(jnp.int32)
    slot = chosen * capacity + rank
    dispatch = (jnp.arange(experts * capacity, dtype=jnp.int32)[:, None] == slot[None, :]).astype(
        low
    )
    scaled = (gate[:, None] * upstream).astype(low)
    both = jnp.concatenate([normed_ffn, scaled], axis=1)
    sent = jnp.dot(dispatch, both, preferred_element_type=jnp.float32).astype(low)
    sent = sent.reshape(experts, capacity, 2 * width)
    sent_mine = pick(sent, core)
    sent_other = swap(pick(sent, 1 - core), size)
    block = jnp.concatenate([sent_mine, sent_other], axis=0)
    arrived = lax.all_gather(block, "shard", axis=0, tiled=True, axis_index_groups=groups)
    batch = arrived[:, :width]
    out_grad = arrived[:, width:]
    before = jnp.dot(batch, in_strip, preferred_element_type=jnp.float32)
    active_wide, pull = jax.vjp(gelu_tanh, before)
    active = active_wide.astype(low)
    returned = jnp.dot(active, out_strip, preferred_element_type=jnp.float32)
    active_grad = jnp.einsum("cd,fd->cf", out_grad, out_strip, preferred_element_type=jnp.float32)
    before_grad = pull(active_grad)[0].astype(low)
    batch_grad = jnp.einsum("cf,df->cd", before_grad, in_strip, preferred_element_type=jnp.float32)
    partial = jnp.concatenate([returned.astype(low), batch_grad.astype(low)], axis=1)
    summed = lax.psum_scatter(
        partial, "shard", scatter_dimension=0, tiled=True, axis_index_groups=groups
    )
    back_mine = summed[:capacity]
    back_other = swap(summed[capacity:], size)
    back = pair_order(core, back_mine, back_other, 0)

    in_grad = jnp.einsum("cd,cf->df", batch, before_grad, preferred_element_type=jnp.float32)
    outer_grad = jnp.einsum("cf,cd->fd", active, out_grad, preferred_element_type=jnp.float32)
    in_grad = lax.all_to_all(
        in_grad.astype(low).reshape(chips, 2 * rows, strip),
        "shard",
        0,
        0,
        axis_index_groups=groups,
        tiled=True,
    )
    in_grad = rep_sum(in_grad, reps)
    in_grad = jnp.transpose(in_grad, (1, 0, 2)).reshape(2, rows, hidden_units)
    grad_mine = pick(in_grad, core)
    grad_other = swap(pick(in_grad, 1 - core).astype(low), size).astype(jnp.float32)
    expert_in_grad = pair_order(core, grad_mine[None], grad_other[None], 0)
    outer_grad = rep_sum(outer_grad.astype(low), reps).reshape(2, strip // 2, width)
    outer_mine = pick(outer_grad, core)
    outer_other = swap(pick(outer_grad, 1 - core).astype(low), size).astype(jnp.float32)
    expert_out_grad = pair_order(core, outer_mine[None], outer_other[None], 0)

    gathered_all = jnp.einsum("st,sd->td", dispatch, back, preferred_element_type=jnp.float32)
    gathered = gathered_all[:, :width]
    ffn_normed_grad = gathered_all[:, width:]
    layer_out = (hidden + gate[:, None] * gathered).astype(low)
    gate_grad = jnp.sum(upstream * gathered, axis=1)
    prob_grad = jnp.where(picked, gate_grad[:, None], 0.0)
    logit_grad = gate_probs * (prob_grad - jnp.sum(gate_probs * prob_grad, axis=1, keepdims=True))
    normed_wide = normed_ffn.astype(jnp.float32)
    router_grad = jnp.einsum("td,te->de", normed_wide, logit_grad, precision=highest)
    ffn_normed_grad = ffn_normed_grad + jnp.einsum(
        "te,de->td", logit_grad, full_router.astype(jnp.float32), precision=highest
    )
    norm_pull = jax.vjp(rms_norm, hidden, gain_ffn)[1]
    hidden_from_norm, gain_ffn_grad = norm_pull(ffn_normed_grad)
    hidden_grad = upstream + hidden_from_norm
    attn_grad = hidden_grad.astype(low)
    attn_out_grad = jnp.einsum("td,te->de", context, attn_grad, preferred_element_type=jnp.float32)
    context_grad = jnp.einsum("te,de->td", attn_grad, full_out, preferred_element_type=jnp.float32)
    context_grad = context_grad.astype(low).reshape(length, heads, head_size)
    prob_grad_attn = jnp.einsum(
        "qhc,khc->hqk", context_grad, values, preferred_element_type=jnp.float32
    )
    value_grad = jnp.einsum(
        "hqk,qhc->khc", probs_low, context_grad, preferred_element_type=jnp.float32
    )
    score_grad = probs * (prob_grad_attn - jnp.sum(probs * prob_grad_attn, axis=-1, keepdims=True))
    offset_grad = pairs_to_offsets(score_grad, length)
    table_grad = jnp.einsum("ho,ob->bh", offset_grad, offset_onehot, precision=highest)
    score_low = score_grad.astype(low)
    query_grad = (
        jnp.einsum("hqk,khc->qhc", score_low, keys, preferred_element_type=jnp.float32) * 0.125
    )
    key_grad = (
        jnp.einsum("hqk,qhc->khc", score_low, query, preferred_element_type=jnp.float32) * 0.125
    )
    projected_grad = jnp.stack(
        [
            query_grad.reshape(length, width),
            key_grad.reshape(length, width),
            value_grad.reshape(length, width),
        ]
    ).astype(low)
    attn_in_grad = jnp.einsum(
        "td,kte->kde", normed, projected_grad, preferred_element_type=jnp.float32
    )
    normed_grad = jnp.einsum(
        "kte,kde->td", projected_grad, full_in, preferred_element_type=jnp.float32
    )
    input_pull = jax.vjp(rms_norm, inputs, gain_attn)[1]
    input_from_norm, gain_attn_grad = input_pull(normed_grad)
    input_grad = hidden_grad + input_from_norm
    gains_grad = jnp.stack([gain_attn_grad, gain_ffn_grad])

    def spread(values):
        flat = values.astype(low).reshape(size, 1, -1)
        return jnp.pad(flat, ((0, 0), (0, 0), (0, width - flat.shape[2])))

    grads = jnp.concatenate(
        [
            jnp.transpose(attn_in_grad.astype(low).reshape(3, size, rows, width), (1, 0, 2, 3)).reshape(
                size, 3 * rows, width
            ),
            attn_out_grad.astype(low).reshape(size, rows, width),
            spread(jnp.transpose(gains_grad.reshape(2, size, rows), (1, 0, 2))),
            spread(router_grad),
            spread(table_grad),
            jnp.zeros((size, extra, width), low),
        ],
        axis=1,
    ).reshape(chips, 2, depth, width)
    kept = pick(grads, core, 1)
    given = swap(pick(grads, 1 - core, 1), size)
    kept = (kept.astype(jnp.float32) + given.astype(jnp.float32)).astype(low)
    mine = lax.psum_scatter(
        kept.reshape(chips * depth, width),
        "shard",
        scatter_dimension=0,
        tiled=True,
        axis_index_groups=groups,
    )
    mine = rep_sum(mine, reps)
    in_shard = mine[: 3 * rows].reshape(3, rows, width)
    out_shard = mine[3 * rows : 4 * rows]
    gains_shard = mine[spot, : 2 * rows].reshape(2, rows)
    router_shard = mine[spot + 1, : experts * rows].reshape(rows, experts)
    table_shard = mine[spot + 2, : table_rows * heads].reshape(table_rows, heads)
    return (
        layer_out,
        input_grad,
        in_shard,
        out_shard,
        gains_shard,
        router_shard,
        table_shard,
        expert_in_grad,
        expert_out_grad,
    )


def solution(mesh):
    placed = (
        P(("rep", "shard"), None),
        P(("rep", "shard"), None),
        P(("rep", "shard"), None),
        P(("rep", "shard"), None),
        P(),
        P(None, "shard", None),
        P("shard", None),
        P(None, "shard"),
        P("shard", None),
        P("shard", None),
        P(None, "shard", None),
        P(None, "shard", None),
    )
    return jax.shard_map(
        functools.partial(shards, mesh.shape["shard"], mesh.shape["rep"]),
        mesh=mesh,
        in_specs=placed,
        out_specs=(
            P(("rep", "shard"), None),
            P(("rep", "shard"), None),
            P(None, "shard", None),
            P("shard", None),
            P(None, "shard"),
            P("shard", None),
            P("shard", None),
            P(None, "shard", None),
            P(None, "shard", None),
        ),
        check_vma=False,
    )
```

time: 1300 us -> 494 us (0.38)
  waiting for transfers between devices: 1020 us -> 283 us
  blocking collectives: 123 us -> 0 us
  local copies, waits for them, and re-layouts: 51.6 us -> 110 us
  matrix products: 72.4 us -> 43.4 us
  starting transfers between devices: 0.61 us -> 14.1 us
    reduce_scatter x5 -> x1, waiting for transfers between devices: 522 us -> 22.7 us  [shards(): lax.psum_scatter(kept.reshape(chips * depth, width), 'shard', scatter_dim...]
    all_gather x6 -> x2, waiting for transfers between devices: 219 us -> 99 us  [the longest x1 56.8 us: shards(): lax.all_gather(packed, 'shard', axis=0, tiled=False, axis_index_groups=gr...]
    unnamed x18 -> x5, waiting for transfers between devices: 201 us -> 82.8 us
    psum x1 -> x0, waiting for transfers between devices: 81.5 us -> none  [shards(): lax.psum((in_shard, out_shard, gains_shard, router_shard, table_shard, ex...]
    all_gather x3 -> x0, blocking collectives: 59.6 us -> none  [the longest x1 23.2 us: shards(): lax.all_gather(gains, 'shard', axis=1, tiled=True)]
    unnamed x1 -> x0, blocking collectives: 57.6 us -> none
    all_to_all x0 -> x2, waiting for transfers between devices: none -> 51.6 us  [the longest x1 26.1 us: shards(): lax.all_to_all(in_grad.astype(low).reshape(chips, 2 * rows, strip), 'shar...]
    concatenate x0 -> x5, local copies, waits for them, and re-layouts: none -> 28.6 us  [the longest x4 26.7 us: shards(): jnp.concatenate([jnp.transpose(attn_in_grad.astype(low).reshape(3, size,...]
  transfers between devices with their start and end apart: 15 -> 17, of which waited for: 13 -> 14; matrix products, arithmetic and copies ran while one was open for 6% -> 5% of each run, Pallas kernels for 0% -> 0%
where the time goes in v1:
time: 494 us; the launch traced here: 491 us
  waiting for transfers between devices  283 us (57%)
  local copies, waits for them, and re-layouts  110 us (22%)
  matrix products  43.4 us (9%)
  other arithmetic  25.8 us (5%)
  between operations  14.6 us (3%)
  starting transfers between devices  14.1 us (3%)
    unnamed x5, waiting for transfers between devices  82.8 us
    all_gather x1, waiting for transfers between devices, shards(): lax.all_gather(packed, 'shard', axis=0, tiled=False, axis_index_groups=gr...  56.8 us
    all_gather x1, waiting for transfers between devices, shards(): lax.all_gather(block, 'shard', axis=0, tiled=True, axis_index_groups=groups)  42.2 us
    concatenate x4, local copies, waits for them, and re-layouts, shards(): jnp.concatenate([jnp.transpose(attn_in_grad.astype(low).reshape(3, size,...  26.7 us
    all_to_all x1, waiting for transfers between devices, shards(): lax.all_to_all(in_grad.astype(low).reshape(chips, 2 * rows, strip), 'shar...  26.1 us
    all_to_all x1, waiting for transfers between devices, shards(): lax.all_to_all(in_rows, 'shard', 0, 0, axis_index_groups=groups, tiled=True)  25.5 us
    unnamed x116, local copies, waits for them, and re-layouts  24 us
    reduce_scatter x1, waiting for transfers between devices, shards(): lax.psum_scatter(kept.reshape(chips * depth, width), 'shard', scatter_dim...  22.7 us
  transfers between devices with their start and end apart: 17, of which 14 were waited for; matrix products, arithmetic and copies ran while one was open for 5% of the time, Pallas kernels for 0%

profile of v1, /device:TPU:0, one launch (start us, length us, event | category | flops | bytes accessed | tf_op | source)
XLA Modules:
  0.0 490.9 jit_solution(17355315705022680317)
XLA Ops:
  12.4 56.8 %all-gather.6.cloned.1.call-done = bf16[1664,768]{1,0:T(8,128)(2,1)} async-done(((bf16[208,768]{1,0:T(8,128)(2,1)}), bf16[1664,768]{1,0:T(8,128)(2,1)}) %all-gather.6.cloned.1.call-update) | async-done | bytes 2555920 | tf_op jit(solution)/shard_map/all_gather | solution.py:113
  87.9 3.9 reshape.241
  97.3 6.8 %rev.13 = f32[12,128,128]{1,2,0:T(8,128)} reverse(f32[12,128,128]{1,2,0:T(8,128)} %copy.143), dimensions={2} | reverse | bytes 1572864 | tf_op jit(solution)/shard_map/rev | solution.py:30
  121.4 4.2 all-to-all-start
  130.4 25.5 %all-to-all-done = bf16[8,96,384]{2,1,0:T(8,128)(2,1)} async-done(((bf16[8,96,384]{2,1,0:T(8,128)(2,1)}), bf16[8,96,384]{2,1,0:T(8,128)(2,1)}, u32[]{:S(2)}, u32[]{:S(2)}) %all-to-all-start) | async-done | bytes 589856 | tf_op jit(solution)/shard_map/all_to_all | solution.py:132
  155.8 42.2 %all-gather.4.cloned.1.call-done = bf16[1280,1536]{1,0:T(8,128)(2,1)} async-done(((bf16[160,1536]{1,0:T(8,128)(2,1)}), bf16[1280,1536]{1,0:T(8,128)(2,1)}) %all-gather.4.cloned.1.call-update) | async-done | bytes 3932176 | tf_op jit(solution)/shard_map/all_gather | solution.py:192
  198.1 2.9 fusion.17
  211.5 6.3 %copy.141 = bf16[1280,1536]{1,0:T(8,128)(2,1)} copy(bf16[1280,1536]{0,1:T(8,128)(2,1)} %pad_maximum_fusion.1) | data formatting | bytes 7864320
  217.8 82.8 %reduce-scatter.7.cloned.1.call-done = bf16[160,1536]{1,0:T(8,128)(2,1)} async-done(((bf16[1280,1536]{1,0:T(8,128)(2,1)}), bf16[160,1536]{1,0:T(8,128)(2,1)}) %reduce-scatter.7.cloned.1.call-update) | async-done | bytes 491536
  315.6 2.5 convolution_convert_fusion.6
  322.7 6.8 %rev.14 = f32[12,128,128]{1,2,0:T(8,128)} reverse(f32[12,128,128]{1,2,0:T(8,128)} %copy-done.1), dimensions={2} | reverse | bytes 1572864 | tf_op jit(solution)/shard_map/rev | solution.py:35
  329.5 2.6 convolution_convert_fusion.4
  337.4 3.3 fusion.40
  340.8 3.0 convolution_convert_fusion.3
  347.7 3.4 reshape.253
  356.9 24.8 %concatenate.55 = bf16[8,2,208,768]{3,2,1,0:T(8,128)(2,1)} concatenate(bf16[8,2,144,768]{3,2,1,0:T(8,128)(2,1)S(1)} %bitcast.143, bf16[8,2,48,768]{3,2,1,0:T(8,128)(2,1)} %bitcast.151, bf16[8,2,1,768]{3,2,1,0:T(2,128)(2,1)} %concatenate.58, bf16[8,2,1,768]{3,2,1,0:T(2,128)(2,1)} %concatenate.59, bf16[8,2,1,768]{3,2,1,0:T(2,128)(2,1)} %concatenate.60, ...), dimensions={2} | concatenate | bytes 10223616 | tf_op jit(solution)/shard_map/concatenate | solution.py:287
  384.2 4.5 collective-permute-done.5
  392.1 3.7 fusion.20
  395.8 4.3 all-to-all-start.1
  400.1 2.6 fusion.23
  404.3 26.1 %all-to-all-done.1 = bf16[8,96,384]{2,1,0:T(8,128)(2,1)S(1)} async-done(((bf16[8,96,384]{2,1,0:T(8,128)(2,1)}), bf16[8,96,384]{2,1,0:T(8,128)(2,1)S(1)}, u32[]{:S(2)}, u32[]{:S(2)}) %all-to-all-start.1) | async-done | bytes 589856 | tf_op jit(solution)/shard_map/all_to_all | solution.py:212
  432.3 11.8 %collective-permute-done.7 = bf16[8,96,384]{2,1,0:T(8,128)(2,1)S(1)} collective-permute-done((bf16[8,96,384]{2,1,0:T(8,128)(2,1)S(1)}, bf16[8,96,384]{2,1,0:T(8,128)(2,1)S(1)}, u32[]{:S(2)}, u32[]{:S(2)}) %collective-permute-start.7) | collective-permute-done | bytes 589856 | tf_op jit(solution)/shard_map/ppermute | solution.py:54
  448.6 22.7 %reduce-scatter.5.cloned.1.call-done = bf16[208,768]{1,0:T(8,128)(2,1)} async-done(((bf16[1664,768]{1,0:T(8,128)(2,1)}), bf16[208,768]{1,0:T(8,128)(2,1)}) %reduce-scatter.5.cloned.1.call-update) | async-done | bytes 319504 | tf_op jit(solution)/shard_map/reduce_scatter | solution.py:303
  473.8 6.0 %collective-permute-done.6 = bf16[208,768]{1,0:T(8,128)(2,1)S(1)} collective-permute-done((bf16[208,768]{1,0:T(8,128)(2,1)}, bf16[208,768]{1,0:T(8,128)(2,1)S(1)}, u32[]{:S(2)}, u32[]{:S(2)}) %collective-permute-start.6) | collective-permute-done | bytes 319520 | tf_op jit(solution)/shard_map/ppermute | solution.py:54
  (263 shorter events, 116.8 us)
Async XLA Ops:
  7.2 61.9 %all-gather.6.cloned.1.call-start = ((), (), s32[]{:S(2)}) async-start(), calls=%async_computation.6 | async-start | bytes 2875392 | tf_op jit(solution)/shard_map/all_gather | solution.py:113
  12.3 185.8 %all-gather.4.cloned.1.call-start = ((), (), s32[]{:S(2)}) async-start(), calls=%async_computation.4 | async-start | bytes 4423680 | tf_op jit(solution)/shard_map/all_gather | solution.py:192
  69.1 5.0 %collective-permute-start = (bf16[8,208,768]{2,1,0:T(8,128)(2,1)}, bf16[8,208,768]{2,1,0:T(8,128)(2,1)S(1)}, u32[]{:S(2)}, u32[]{:S(2)}) collective-permute-start(bf16[8,208,768]{2,1,0:T(8,128)(2,1)} %bitcast.155), channel_id=1, source_target_pairs={{0,1},{1,0},{2,3},{3,2},{4,5},{5,4},{6,7},{7,6},{8,9},{9,8},{10,11... | collective-permute-start | bytes 7667720 | tf_op jit(solution)/shard_map/ppermute | solution.py:43
  71.9 12.6 %copy-start.37 = (f32[128]{0:T(128)}, f32[128]{0:T(128)S(1)}, u32[]{:S(2)}) copy-start(f32[128]{0:T(128)S(1)} %fusion.74) | copy-start | bytes 1540
  114.3 1.6 collective-permute-start.1
  117.7 1.6 collective-permute-start.2
  121.4 34.4 %all-to-all-start = ((bf16[8,96,384]{2,1,0:T(8,128)(2,1)}), bf16[8,96,384]{2,1,0:T(8,128)(2,1)}, u32[]{:S(2)}, u32[]{:S(2)}) async-start(bf16[8,96,384]{2,1,0:T(8,128)(2,1)} %copy.115), calls=%async_computation | async-start | bytes 1179648 | tf_op jit(solution)/shard_map/all_to_all | solution.py:132
  125.6 175.0 %reduce-scatter.7.cloned.1.call-start = ((), (), s32[]{:S(2)}) async-start(), calls=%async_computation.7 | async-start | bytes 4423680
  126.9 1.6 collective-permute-start.3
  217.8 253.5 %reduce-scatter.5.cloned.1.call-start = ((), (), s32[]{:S(2)}) async-start(), calls=%async_computation.5 | async-start | bytes 2875392 | tf_op jit(solution)/shard_map/reduce_scatter | solution.py:303
  304.3 2.1 collective-permute-start.4
  322.7 14.6 %copy-start.38 = (f32[128]{0:T(128)S(1)}, f32[128]{0:T(128)}, u32[]{:S(2)}) copy-start(f32[128]{0:T(128)} %copy-done.37) | copy-start | bytes 1540
  383.8 4.9 collective-permute-start.5
  392.1 8.0 %copy-start.48 = (f32[1280,384]{1,0:T(8,128)S(1)}, f32[1280,384]{1,0:T(8,128)}, u32[]{:S(2)}) copy-start(f32[1280,384]{1,0:T(8,128)} %copy-done.47) | copy-start | bytes 5898244
  395.8 34.6 %all-to-all-start.1 = ((bf16[8,96,384]{2,1,0:T(8,128)(2,1)}), bf16[8,96,384]{2,1,0:T(8,128)(2,1)S(1)}, u32[]{:S(2)}, u32[]{:S(2)}) async-start(bf16[8,96,384]{2,1,0:T(8,128)(2,1)} %bitcast.49), calls=%async_computation.2 | async-start | bytes 1179648 | tf_op jit(solution)/shard_map/all_to_all | solution.py:212
  402.7 28.7 %collective-permute-start.9 = (bf16[384,768]{1,0:T(8,128)(2,1)S(1)}, bf16[384,768]{1,0:T(8,128)(2,1)S(1)}, u32[]{:S(2)}, u32[]{:S(2)}) collective-permute-start(bf16[384,768]{1,0:T(8,128)(2,1)S(1)} %fusion.23), channel_id=1, source_target_pairs={{0,16},{16,0},{1,17},{17,1},{2,18},{18,2},{3,19},{19,3},{4,20},{20... | collective-permute-start | bytes 1769480 | tf_op jit(solution)/shard_map/ppermute | solution.py:54
  430.4 13.7 %collective-permute-start.7 = (bf16[8,96,384]{2,1,0:T(8,128)(2,1)S(1)}, bf16[8,96,384]{2,1,0:T(8,128)(2,1)S(1)}, u32[]{:S(2)}, u32[]{:S(2)}) collective-permute-start(bf16[8,96,384]{2,1,0:T(8,128)(2,1)S(1)} %all-to-all-done.1), channel_id=1, source_target_pairs={{0,16},{16,0},{1,17},{17,1},{2,18},{18,2},{3,19},{19,3},{4,20},{20... | collective-permute-start | bytes 1769480 | tf_op jit(solution)/shard_map/ppermute | solution.py:54
  432.3 12.9 %collective-permute-start.10 = (bf16[192,768]{1,0:T(8,128)(2,1)}, bf16[192,768]{1,0:T(8,128)(2,1)}, u32[]{:S(2)}, u32[]{:S(2)}) collective-permute-start(bf16[192,768]{1,0:T(8,128)(2,1)} %fusion.50), channel_id=1, source_target_pairs={{0,1},{1,0},{2,3},{3,2},{4,5},{5,4},{6,7},{7,6},{8,9},{9,8},{10,11... | collective-permute-start | bytes 884744 | tf_op jit(solution)/shard_map/ppermute | solution.py:43
  445.1 2.2 collective-permute-start.8
  447.4 25.5 %copy-start.41 = (f32[128]{0:T(128)S(1)}, f32[128]{0:T(128)}, u32[]{:S(2)}) copy-start(f32[128]{0:T(128)} %copy-done.40) | copy-start | bytes 1540
  447.4 25.5 %copy-start.6 = (f32[128,768]{1,0:T(8,128)S(1)}, f32[128,768]{1,0:T(8,128)}, u32[]{:S(2)}) copy-start(f32[128,768]{1,0:T(8,128)} %copy-done.5) | copy-start | bytes 1179652
  447.4 25.5 %copy-start.9 = (bf16[128,768]{1,0:T(8,128)(2,1)S(1)}, bf16[128,768]{1,0:T(8,128)(2,1)}, u32[]{:S(2)}) copy-start(bf16[128,768]{1,0:T(8,128)(2,1)} %param.12) | copy-start | bytes 589828
  447.4 25.5 %copy-start.24 = (f32[128,768]{1,0:T(8,128)S(1)}, f32[128,768]{1,0:T(8,128)}, u32[]{:S(2)}) copy-start(f32[128,768]{1,0:T(8,128)} %get-tuple-element.96) | copy-start | bytes 1179652
  471.3 8.4 %collective-permute-start.6 = (bf16[208,768]{1,0:T(8,128)(2,1)}, bf16[208,768]{1,0:T(8,128)(2,1)S(1)}, u32[]{:S(2)}, u32[]{:S(2)}) collective-permute-start(bf16[208,768]{1,0:T(8,128)(2,1)} %reduce-scatter.5.cloned.1.call-done), channel_id=1, source_target_pairs={{0,16},{16,0},{1,17},{17,1},{2,18},{18,2},{3,19},{19,3},{4,20},{20... | collective-permute-start | bytes 958472 | tf_op jit(solution)/shard_map/ppermute | solution.py:54
  (44 other events, 119.2 us)
Sparse Core Ops, SparseCore 0:
  12.4 56.6 all-gather.5
  116.8 81.2 all-gather.3
  217.9 82.6 reduce-scatter.6
  391.0 80.2 reduce-scatter.4

commit v2 on v1

--- a/solution.py
+++ b/solution.py
@@ -3,6 +3,8 @@
 import jax
 import jax.numpy as jnp
 from jax import lax
+from jax.experimental import pallas as pl
+from jax.experimental.pallas import tpu as pltpu
 from jax.sharding import PartitionSpec as P
 
 BUCKETS = 32
@@ -63,6 +65,207 @@
 def pad_row(values, width):
     flat = values.reshape(-1)
     return jnp.pad(flat, (0, width - flat.shape[0])).reshape(1, width)
+
+
+def grid_of(size):
+    chips = size // 2
+    outer = 4 if chips % 4 == 0 else 1
+    return outer, chips // outer
+
+
+def place_of(size):
+    outer, inner = grid_of(size)
+    me = lax.axis_index("shard")
+    core = lax.rem(me, 2)
+    chip = lax.div(me, 2)
+    z = lax.div(chip, inner)
+    y = lax.rem(chip, inner)
+
+    def device(far, near):
+        return {"shard": (far * inner + near) * 2 + core}
+
+    return z, y, device
+
+
+def greet(size):
+    outer, inner = grid_of(size)
+    z, y, device = place_of(size)
+    barrier = pltpu.get_barrier_semaphore()
+    for d in range(1, outer):
+        pl.semaphore_signal(
+            barrier,
+            inc=1,
+            device_id=device(lax.rem(z + d, outer), y),
+            device_id_type=pl.DeviceIdType.MESH,
+        )
+    for e in range(1, inner):
+        pl.semaphore_signal(
+            barrier,
+            inc=1,
+            device_id=device(z, lax.rem(y + e, inner)),
+            device_id_type=pl.DeviceIdType.MESH,
+        )
+    pl.semaphore_wait(barrier, outer + inner - 2)
+
+
+def send(src, dst, send_sem, recv_sem, target):
+    copy = pltpu.make_async_remote_copy(
+        src_ref=src,
+        dst_ref=dst,
+        send_sem=send_sem,
+        recv_sem=recv_sem,
+        device_id=target,
+        device_id_type=pl.DeviceIdType.MESH,
+    )
+    copy.start()
+    return copy
+
+
+def gather_kernel(size, x_ref, o_ref, own_sem, z_send, z_recv, y_send, y_recv):
+    outer, inner = grid_of(size)
+    z, y, device = place_of(size)
+    chip = z * inner + y
+    greet(size)
+    own = pltpu.make_async_copy(x_ref, o_ref.at[chip], own_sem)
+    own.start()
+    along = []
+    for d in range(1, outer):
+        target = device(lax.rem(z + d, outer), y)
+        along.append(send(x_ref, o_ref.at[chip], z_send.at[d - 1], z_recv.at[d - 1], target))
+    across = []
+    for e in range(1, inner):
+        target = device(z, lax.rem(y + e, inner))
+        across.append(send(x_ref, o_ref.at[chip], y_send.at[0, e - 1], y_recv.at[0, e - 1], target))
+    for d in range(1, outer):
+        along[d - 1].wait_recv()
+        source = lax.rem(z + outer - d, outer) * inner + y
+        for e in range(1, inner):
+            target = device(z, lax.rem(y + e, inner))
+            across.append(
+                send(
+                    o_ref.at[source],
+                    o_ref.at[source],
+                    y_send.at[d, e - 1],
+                    y_recv.at[d, e - 1],
+                    target,
+                )
+            )
+    own.wait()
+    for copy in across:
+        copy.wait_recv()
+    for copy in along + across:
+        copy.wait_send()
+
+
+def gather_chips(block, size, collective_id):
+    outer, inner = grid_of(size)
+    return pl.pallas_call(
+        functools.partial(gather_kernel, size),
+        out_shape=jax.ShapeDtypeStruct((size // 2,) + block.shape, block.dtype),
+        in_specs=[pl.BlockSpec(memory_space=pltpu.VMEM)],
+        out_specs=pl.BlockSpec(memory_space=pltpu.VMEM),
+        scratch_shapes=[
+            pltpu.SemaphoreType.DMA,
+            pltpu.SemaphoreType.DMA((max(outer - 1, 1),)),
+            pltpu.SemaphoreType.DMA((max(outer - 1, 1),)),
+            pltpu.SemaphoreType.DMA((outer, max(inner - 1, 1))),
+            pltpu.SemaphoreType.DMA((outer, max(inner - 1, 1))),
+        ],
+        compiler_params=pltpu.CompilerParams(
+            collective_id=collective_id, has_side_effects=True, vmem_limit_bytes=40 << 20
+        ),
+    )(block)
+
+
+def scatter_kernel(
+    size, p_ref, o_ref, y_buf, z_out, z_in, total, y_send, y_recv, z_send, z_recv
+):
+    outer, inner = grid_of(size)
+    z, y, device = place_of(size)
+    rows = o_ref.shape[0]
+    step = 16
+    greet(size)
+    across = {}
+    order = [*range(1, outer), 0]
+    for d in order:
+        far = lax.rem(z + d, outer)
+        for e in range(1, inner):
+            near = lax.rem(y + e, inner)
+            across[d, e] = send(
+                p_ref.at[far * inner + near],
+                y_buf.at[e - 1, d],
+                y_send.at[d, e - 1],
+                y_recv.at[d, e - 1],
+                device(z, near),
+            )
+    along = []
+    for d in order:
+        far = lax.rem(z + d, outer)
+        for e in range(1, inner):
+            across[d, e].wait_recv()
+
+        def add(i, carry):
+            at = pl.ds(pl.multiple_of(i * step, step), step)
+            value = p_ref[far * inner + y, at].astype(jnp.float32)
+            for e in range(1, inner):
+                value = value + y_buf[e - 1, d, at].astype(jnp.float32)
+            if d == 0:
+                total[at] = value
+            else:
+                z_out[d - 1, at] = value.astype(z_out.dtype)
+            return carry
+
+        lax.fori_loop(0, rows // step, add, 0)
+        if d > 0:
+            along.append(
+                send(
+                    z_out.at[d - 1],
+                    z_in.at[d - 1],
+                    z_send.at[d - 1],
+                    z_recv.at[d - 1],
+                    device(far, y),
+                )
+            )
+    for copy in along:
+        copy.wait_recv()
+
+    def finish(i, carry):
+        at = pl.ds(pl.multiple_of(i * step, step), step)
+        value = total[at]
+        for d in range(1, outer):
+            value = value + z_in[d - 1, at].astype(jnp.float32)
+        o_ref[at] = value.astype(o_ref.dtype)
+        return carry
+
+    lax.fori_loop(0, rows // step, finish, 0)
+    for copy in [*along, *across.values()]:
+        copy.wait_send()
+
+
+def scatter_chips(partial, size, collective_id):
+    outer, inner = grid_of(size)
+    rows, width = partial.shape[1:]
+    steps = max(outer - 1, 1)
+    sides = max(inner - 1, 1)
+    return pl.pallas_call(
+        functools.partial(scatter_kernel, size),
+        out_shape=jax.ShapeDtypeStruct((rows, width), partial.dtype),
+        in_specs=[pl.BlockSpec(memory_space=pltpu.VMEM)],
+        out_specs=pl.BlockSpec(memory_space=pltpu.VMEM),
+        scratch_shapes=[
+            pltpu.VMEM((sides, outer, rows, width), partial.dtype),
+            pltpu.VMEM((steps, rows, width), partial.dtype),
+            pltpu.VMEM((steps, rows, width), partial.dtype),
+            pltpu.VMEM((rows, width), jnp.float32),
+            pltpu.SemaphoreType.DMA((outer, sides)),
+            pltpu.SemaphoreType.DMA((outer, sides)),
+            pltpu.SemaphoreType.DMA((steps,)),
+            pltpu.SemaphoreType.DMA((steps,)),
+        ],
+        compiler_params=pltpu.CompilerParams(
+            collective_id=collective_id, has_side_effects=True, vmem_limit_bytes=48 << 20
+        ),
+    )(partial)
 
 
 def shards(
@@ -96,6 +299,23 @@
     groups = [[2 * j + c for j in range(chips)] for c in range(2)]
     core = lax.axis_index("shard") % 2
 
+    places = jnp.arange(length, dtype=jnp.int32)
+    chosen = routes[:, 0]
+    picked = chosen[:, None] == jnp.arange(experts, dtype=jnp.int32)[None, :]
+    earlier = (places[None, :] < places[:, None]).astype(low)
+    ranks = jnp.dot(earlier, picked.astype(low), preferred_element_type=jnp.float32)
+    rank = jnp.sum(jnp.where(picked, ranks, 0.0), axis=1).astype(jnp.int32)
+    slot = chosen * capacity + rank
+    dispatch = (jnp.arange(experts * capacity, dtype=jnp.int32)[:, None] == slot[None, :]).astype(
+        low
+    )
+    up_sent = jnp.dot(dispatch, cotangent, preferred_element_type=jnp.float32).astype(low)
+    up_sent = up_sent.reshape(experts, capacity, width)
+    up_mine = pick(up_sent, core)
+    up_other = swap(pick(up_sent, 1 - core), size)
+    up_block = jnp.concatenate([up_mine, up_other], axis=0)
+    up_slots = lax.all_gather(up_block, "shard", axis=0, tiled=True, axis_index_groups=groups)
+
     packed = jnp.concatenate(
         [
             attn_in.reshape(3 * rows, width),
@@ -110,7 +330,7 @@
     extra = -depth % 16
     packed = jnp.pad(packed, ((0, extra), (0, 0)))
     depth = depth + extra
-    same = lax.all_gather(packed, "shard", axis=0, tiled=False, axis_index_groups=groups)
+    same = gather_chips(packed, size, 0)
     other = swap(same, size)
     whole = jnp.stack(
         [jnp.where(core == 0, same, other), jnp.where(core == 0, other, same)], axis=1
@@ -147,7 +367,6 @@
     query = projected[0].reshape(length, heads, head_size)
     keys = projected[1].reshape(length, heads, head_size)
     values = projected[2].reshape(length, heads, head_size)
-    places = jnp.arange(length, dtype=jnp.int32)
     offset_onehot = (
         bucket_ids[:, None] == jnp.arange(bucket_count, dtype=jnp.int32)[None, :]
     ).astype(jnp.float32)
@@ -172,26 +391,16 @@
     normed_ffn = rms_norm(hidden, gain_ffn).astype(low)
     logits = jnp.dot(normed_ffn, full_router, preferred_element_type=jnp.float32)
     gate_probs = jax.nn.softmax(logits, axis=-1)
-    chosen = routes[:, 0]
-    picked = chosen[:, None] == jnp.arange(experts, dtype=jnp.int32)[None, :]
     gate = jnp.sum(jnp.where(picked, gate_probs, 0.0), axis=1)
-    earlier = (places[None, :] < places[:, None]).astype(low)
-    ranks = jnp.dot(earlier, picked.astype(low), preferred_element_type=jnp.float32)
-    rank = jnp.sum(jnp.where(picked, ranks, 0.0), axis=1).astype(jnp.int32)
-    slot = chosen * capacity + rank
-    dispatch = (jnp.arange(experts * capacity, dtype=jnp.int32)[:, None] == slot[None, :]).astype(
-        low
-    )
-    scaled = (gate[:, None] * upstream).astype(low)
-    both = jnp.concatenate([normed_ffn, scaled], axis=1)
-    sent = jnp.dot(dispatch, both, preferred_element_type=jnp.float32).astype(low)
-    sent = sent.reshape(experts, capacity, 2 * width)
+    sent = jnp.dot(dispatch, normed_ffn, preferred_element_type=jnp.float32).astype(low)
+    sent = sent.reshape(experts, capacity, width)
     sent_mine = pick(sent, core)
     sent_other = swap(pick(sent, 1 - core), size)
     block = jnp.concatenate([sent_mine, sent_other], axis=0)
-    arrived = lax.all_gather(block, "shard", axis=0, tiled=True, axis_index_groups=groups)
-    batch = arrived[:, :width]
-    out_grad = arrived[:, width:]
+    batch = gather_chips(block, size, 1).reshape(2 * chips * capacity, width)
+    slot_logits = jnp.dot(batch, full_router, preferred_element_type=jnp.float32)
+    slot_gate = pick(jax.nn.softmax(slot_logits, axis=-1), core, 1)
+    out_grad = (slot_gate[:, None] * up_slots.astype(jnp.float32)).astype(low)
     before = jnp.dot(batch, in_strip, preferred_element_type=jnp.float32)
     active_wide, pull = jax.vjp(gelu_tanh, before)
     active = active_wide.astype(low)
@@ -200,9 +409,7 @@
     before_grad = pull(active_grad)[0].astype(low)
     batch_grad = jnp.einsum("cf,df->cd", before_grad, in_strip, preferred_element_type=jnp.float32)
     partial = jnp.concatenate([returned.astype(low), batch_grad.astype(low)], axis=1)
-    summed = lax.psum_scatter(
-        partial, "shard", scatter_dimension=0, tiled=True, axis_index_groups=groups
-    )
+    summed = scatter_chips(partial.reshape(chips, 2 * capacity, 2 * width), size, 2)
     back_mine = summed[:capacity]
     back_other = swap(summed[capacity:], size)
     back = pair_order(core, back_mine, back_other, 0)
@@ -300,13 +507,7 @@
     kept = pick(grads, core, 1)
     given = swap(pick(grads, 1 - core, 1), size)
     kept = (kept.astype(jnp.float32) + given.astype(jnp.float32)).astype(low)
-    mine = lax.psum_scatter(
-        kept.reshape(chips * depth, width),
-        "shard",
-        scatter_dimension=0,
-        tiled=True,
-        axis_index_groups=groups,
-    )
+    mine = scatter_chips(kept, size, 3)
     mine = rep_sum(mine, reps)
     in_shard = mine[: 3 * rows].reshape(3, rows, width)
     out_shard = mine[3 * rows : 4 * rows]

time: 494 us -> 411 us (0.83)
  waiting for transfers between devices: 283 us -> 20.1 us
  Pallas kernels: 0 us -> 187 us
  local copies, waits for them, and re-layouts: 110 us -> 95.9 us
  starting transfers between devices: 14.1 us -> 23.3 us
    pallas_call x0 -> x4, Pallas kernels: none -> 187 us  [the longest x2 97.2 us: scatter_chips(): pl.pallas_call(functools.partial(scatter_kernel, size), out_shape=jax.Sha...]
    all_gather x2 -> x1, waiting for transfers between devices: 99 us -> 0.01 us  [shards(): lax.all_gather(up_block, 'shard', axis=0, tiled=True, axis_index_groups=g...]
    unnamed x5 -> x1, waiting for transfers between devices: 82.8 us -> 0.02 us
    all_to_all x1, waiting for transfers between devices: 26.1 us -> 0.01 us  [shards(): lax.all_to_all(in_grad.astype(low).reshape(chips, 2 * rows, strip), 'shar...]
    all_to_all x1, waiting for transfers between devices: 25.5 us -> 0.01 us  [shards(): lax.all_to_all(in_rows, 'shard', 0, 0, axis_index_groups=groups, tiled=True)]
    reduce_scatter x1 -> x0, waiting for transfers between devices: 22.7 us -> none  [shards(): lax.psum_scatter(kept.reshape(chips * depth, width), 'shard', scatter_dim...]
    ppermute x8 -> x9, waiting for transfers between devices: 9.15 us -> 1.35 us  [swap(): return lax.ppermute(array, 'shard', [(i, i ^ 1) for i in range(size)])]
    unnamed x116 -> x145, local copies, waits for them, and re-layouts: 24 us -> 16.9 us
  transfers between devices with their start and end apart: 17 -> 15, of which waited for: 14 -> 4; matrix products, arithmetic and copies ran while one was open for 5% -> 33% of each run, Pallas kernels for 0% -> 36%
where the time goes in v2:
time: 411 us; the launch traced here: 409 us
  Pallas kernels  187 us (45%)
  local copies, waits for them, and re-layouts  95.9 us (23%)
  matrix products  39.1 us (10%)
  other arithmetic  28.6 us (7%)
  starting transfers between devices  23.3 us (6%)
  waiting for transfers between devices  20.1 us (5%)
  between operations  15.2 us (4%)
    pallas_call x2, Pallas kernels, scatter_chips(): pl.pallas_call(functools.partial(scatter_kernel, size), out_shape=jax.Sha...  97.2 us
    pallas_call x2, Pallas kernels, gather_chips(): pl.pallas_call(functools.partial(gather_kernel, size), out_shape=jax.Shap...  89.5 us
    concatenate x9, local copies, waits for them, and re-layouts, shards(): jnp.concatenate([jnp.transpose(attn_in_grad.astype(low).reshape(3, size,...  31.4 us
    ppermute x3, waiting for transfers between devices, rep_sum(): other = lax.ppermute(array, 'rep', [(0, 1), (1, 0)])  18.8 us
    unnamed x145, local copies, waits for them, and re-layouts  16.9 us
    all_to_all x1, starting transfers between devices, shards(): lax.all_to_all(in_rows, 'shard', 0, 0, axis_index_groups=groups, tiled=True)  10.1 us
    all_to_all x1, starting transfers between devices, shards(): lax.all_to_all(in_grad.astype(low).reshape(chips, 2 * rows, strip), 'shar...  8.77 us
  transfers between devices with their start and end apart: 15, of which 4 were waited for; matrix products, arithmetic and copies ran while one was open for 33% of the time, Pallas kernels for 36%

profile of v2, /device:TPU:0, one launch (start us, length us, event | category | flops | bytes accessed | tf_op | source)
XLA Modules:
  0.0 409.0 jit_solution(18390097415629948684)
XLA Ops:
  15.5 43.2 %shard_map.187 = bf16[8,208,768]{2,1,0:T(8,128)(2,1)S(1)} custom-call(bf16[208,768]{1,0:T(8,128)(2,1)S(1)} %pad.37.x_ref), custom_call_target="tpu_custom_call" | custom-call | tf_op jit(solution)/shard_map/pallas_call | solution.py:162
  66.8 10.1 %all-to-all-start = ((bf16[8,96,384]{2,1,0:T(8,128)(2,1)}), bf16[8,96,384]{2,1,0:T(8,128)(2,1)}, u32[]{:S(2)}, u32[]{:S(2)}) async-start(bf16[8,96,384]{2,1,0:T(8,128)(2,1)} %copy.124), calls=%async_computation | async-start | bytes 1179648 | tf_op jit(solution)/shard_map/all_to_all | solution.py:352
  92.8 2.5 reshape.249
  104.0 46.3 %shard_map.188 = bf16[8,160,768]{2,1,0:T(8,128)(2,1)S(1)} custom-call(bf16[160,768]{1,0:T(8,128)(2,1)S(1)} %pad_maximum_fusion.9.x_ref), custom_call_target="tpu_custom_call" | custom-call | tf_op jit(solution)/shard_map/pallas_call | solution.py:162
  155.3 2.7 convolution_convert_fusion.1
  158.0 4.6 %fusion.8 = bf16[1280,384]{1,0:T(8,128)(2,1)S(1)} fusion(f32[1280,384]{1,0:T(8,128)} %copy-done.65, bf16[1280,768]{1,0:T(8,128)(2,1)} %all-gather.2.cloned.1.call-done, f32[1280]{0:T(1024)} %divide_reduce_fusion, bf16[192,768]{1,0:T(8,128)(2,1)} %get-tuple-element.76, bf16[192,768]{1,0:T(8,128)(2,1)} %get-tuple-element.75), kind=kOutput, calls=%fused_computation.20 | convolution fusion | flops 768933888 | bytes 5510144 | tf_op jit(solution)/shard_map/cd,fd->cf/dot_general | solution.py:408
  164.6 3.7 convolution_convert_fusion
  168.3 8.8 %all-to-all-start.1 = ((bf16[8,96,384]{2,1,0:T(8,128)(2,1)}), bf16[8,96,384]{2,1,0:T(8,128)(2,1)}, u32[]{:S(2)}, u32[]{:S(2)}) async-start(bf16[8,96,384]{2,1,0:T(8,128)(2,1)} %bitcast.178), calls=%async_computation.1 | async-start | bytes 1179648 | tf_op jit(solution)/shard_map/all_to_all | solution.py:419
  177.1 3.6 pad_maximum_fusion.1
  180.8 6.3 %copy.125 = bf16[1280,1536]{1,0:T(8,128)(2,1)} copy(bf16[1280,1536]{0,1:T(8,128)(2,1)} %pad_maximum_fusion.1) | data formatting | bytes 7864320 | tf_op jit(solution)/shard_map/concatenate | solution.py:411
  189.1 57.3 %shard_map.189 = bf16[160,1536]{1,0:T(8,128)(2,1)S(1)} custom-call(bf16[8,160,1536]{2,1,0:T(8,128)(2,1)S(1)} %bitcast.144), custom_call_target="tpu_custom_call" | custom-call | tf_op jit(solution)/shard_map/pallas_call | solution.py:250
  255.1 2.6 convolution_convert_fusion.9
  261.0 3.9 rev.14
  264.8 2.7 convolution_convert_fusion.3
  276.4 2.3 copy.154
  280.5 3.8 fusion.25
  285.2 2.4 copy.140
  289.3 3.4 reshape.264
  298.2 24.7 %concatenate.55 = bf16[8,2,208,768]{3,2,0,1:T(8,128)(2,1)} concatenate(bf16[8,2,144,768]{3,2,0,1:T(8,128)(2,1)S(1)} %copy.139, bf16[8,2,48,768]{3,2,0,1:T(8,128)(2,1)} %copy.140, bf16[8,2,1,768]{3,2,0,1:T(2,128)(2,1)} %copy.141, bf16[8,2,1,768]{3,2,0,1:T(2,128)(2,1)} %copy.142, bf16[8,2,1,768]{3,2,0,1:T(2,128)(2,1)} %copy.143, bf16[8,2,13,768]{3,2,0,1:T(8,128)(2,1)} %broadcast_in_dim.69), dimensions={2} | concatenate | bytes 10223616 | tf_op jit(solution)/shard_map/concatenate | solution.py:494
  323.0 3.5 dynamic-slice_bitcast_fusion
  330.5 12.0 %collective-permute-done.8 = bf16[8,96,384]{2,1,0:T(8,128)(2,1)S(1)} collective-permute-done((bf16[8,96,384]{2,1,0:T(8,128)(2,1)}, bf16[8,96,384]{2,1,0:T(8,128)(2,1)S(1)}, u32[]{:S(2)}, u32[]{:S(2)}) %collective-permute-start.8) | collective-permute-done | bytes 589856 | tf_op jit(solution)/shard_map/ppermute | solution.py:56
  347.0 3.1 fusion.1.p_ref
  350.2 39.9 %shard_map.190 = bf16[208,768]{1,0:T(8,128)(2,1)S(1)} custom-call(bf16[8,208,768]{2,1,0:T(8,128)(2,1)S(1)} %fusion.1.p_ref), custom_call_target="tpu_custom_call" | custom-call | tf_op jit(solution)/shard_map/pallas_call | solution.py:250
  391.8 6.7 %collective-permute-done.7 = bf16[208,768]{1,0:T(8,128)(2,1)S(1)} collective-permute-done((bf16[208,768]{1,0:T(8,128)(2,1)S(1)}, bf16[208,768]{1,0:T(8,128)(2,1)S(1)}, u32[]{:S(2)}, u32[]{:S(2)}) %collective-permute-start.7) | collective-permute-done | bytes 319520 | tf_op jit(solution)/shard_map/ppermute | solution.py:56
  (300 shorter events, 93.6 us)
Async XLA Ops:
  7.2 150.8 %all-gather.2.cloned.1.call-start = ((), (), s32[]{:S(2)}) async-start(), calls=%async_computation.2 | async-start | bytes 2211840 | tf_op jit(solution)/shard_map/all_gather | solution.py:317
  10.6 51.7 %collective-permute-start.4 = (bf16[80,768]{1,0:T(8,128)(2,1)}, bf16[80,768]{1,0:T(8,128)(2,1)}, u32[]{:S(2)}, u32[]{:S(2)}) collective-permute-start(bf16[80,768]{1,0:T(8,128)(2,1)} %get-tuple-element.87), channel_id=1, source_target_pairs={{0,1},{1,0},{2,3},{3,2},{4,5},{5,4},{6,7},{7,6},{8,9},{9,8},{10,11... | collective-permute-start | bytes 368648 | tf_op jit(solution)/shard_map/ppermute | solution.py:45
  15.4 43.4 %copy-start.30 = (bf16[2,192,768]{2,1,0:T(8,128)(2,1)S(1)}, bf16[2,192,768]{2,1,0:T(8,128)(2,1)}, u32[]{:S(2)}) copy-start(bf16[2,192,768]{2,1,0:T(8,128)(2,1)} %param.23) | copy-start | bytes 1769476
  15.4 44.6 %copy-start.29 = (bf16[2,48,3072]{2,1,0:T(8,128)(2,1)S(1)}, bf16[2,48,3072]{2,1,0:T(8,128)(2,1)}, u32[]{:S(2)}) copy-start(bf16[2,48,3072]{2,1,0:T(8,128)(2,1)} %param.22) | copy-start | bytes 1769476
  15.4 45.3 %copy-start.63 = (s32[1,3]{1,0:T(1,128)S(1)}, s32[1,3]{1,0:T(1,128)}, u32[]{:S(2)}) copy-start(s32[1,3]{1,0:T(1,128)} %param.14) | copy-start | bytes 40
  15.5 45.5 %copy-start.6 = (bf16[128,768]{1,0:T(8,128)(2,1)S(1)}, bf16[128,768]{1,0:T(8,128)(2,1)}, u32[]{:S(2)}) copy-start(bf16[128,768]{1,0:T(8,128)(2,1)} %param.12) | copy-start | bytes 589828
  58.7 20.1 %collective-permute-start = (bf16[8,208,768]{2,1,0:T(8,128)(2,1)S(1)}, bf16[8,208,768]{2,1,0:T(8,128)(2,1)}, u32[]{:S(2)}, u32[]{:S(2)}) collective-permute-start(bf16[8,208,768]{2,1,0:T(8,128)(2,1)S(1)} %shard_map.187), channel_id=1, source_target_pairs={{0,1},{1,0},{2,3},{3,2},{4,5},{5,4},{6,7},{7,6},{8,9},{9,8},{10,11... | collective-permute-start | bytes 7667720 | tf_op jit(solution)/shard_map/ppermute | solution.py:45
  59.5 17.4 %collective-permute-start.3 = (bf16[192,768]{1,0:T(8,128)(2,1)}, bf16[192,768]{1,0:T(8,128)(2,1)}, u32[]{:S(2)}, u32[]{:S(2)}) collective-permute-start(bf16[192,768]{1,0:T(8,128)(2,1)} %dynamic-slice_bitcast_fusion.1), channel_id=1, source_target_pairs={{0,1},{1,0},{2,3},{3,2},{4,5},{5,4},{6,7},{7,6},{8,9},{9,8},{10,11... | collective-permute-start | bytes 884744 | tf_op jit(solution)/shard_map/ppermute | solution.py:45
  60.7 4.0 collective-permute-start.2
  66.8 84.9 %all-to-all-start = ((bf16[8,96,384]{2,1,0:T(8,128)(2,1)}), bf16[8,96,384]{2,1,0:T(8,128)(2,1)}, u32[]{:S(2)}, u32[]{:S(2)}) async-start(bf16[8,96,384]{2,1,0:T(8,128)(2,1)} %copy.124), calls=%async_computation | async-start | bytes 1179648 | tf_op jit(solution)/shard_map/all_to_all | solution.py:352
  102.6 1.4 collective-permute-start.1
  102.9 47.5 %copy-start.17 = (bf16[768,2]{1,0:T(8,128)(2,1)S(1)}, bf16[768,2]{1,0:T(8,128)(2,1)}, u32[]{:S(2)}) copy-start(bf16[768,2]{1,0:T(8,128)(2,1)} %copy-done.16) | copy-start | bytes 9220
  168.3 158.4 %all-to-all-start.1 = ((bf16[8,96,384]{2,1,0:T(8,128)(2,1)}), bf16[8,96,384]{2,1,0:T(8,128)(2,1)}, u32[]{:S(2)}, u32[]{:S(2)}) async-start(bf16[8,96,384]{2,1,0:T(8,128)(2,1)} %bitcast.178), calls=%async_computation.1 | async-start | bytes 1179648 | tf_op jit(solution)/shard_map/all_to_all | solution.py:419
  189.1 57.5 %copy-start.44 = (f32[1280]{0:T(1024)S(1)}, f32[1280]{0:T(1024)}, u32[]{:S(2)}) copy-start(f32[1280]{0:T(1024)} %divide_reduce_fusion) | copy-start | bytes 15364
  189.1 57.5 %copy-start.60 = (bf16[1280,768]{1,0:T(8,128)(2,1)S(1)}, bf16[1280,768]{1,0:T(8,128)(2,1)}, u32[]{:S(2)}) copy-start(bf16[1280,768]{1,0:T(8,128)(2,1)} %all-gather.2.cloned.1.call-done) | copy-start | bytes 5898244
  189.1 57.5 %copy-start.66 = (f32[1280,384]{1,0:T(8,128)S(1)}, f32[1280,384]{1,0:T(8,128)}, u32[]{:S(2)}) copy-start(f32[1280,384]{1,0:T(8,128)} %copy-done.65) | copy-start | bytes 5898244
  246.5 3.9 collective-permute-start.5
  248.8 79.6 %collective-permute-start.10 = (bf16[384,768]{1,0:T(8,128)(2,1)}, bf16[384,768]{1,0:T(8,128)(2,1)}, u32[]{:S(2)}, u32[]{:S(2)}) collective-permute-start(bf16[384,768]{1,0:T(8,128)(2,1)} %convolution_convert_fusion.4), channel_id=1, source_target_pairs={{0,16},{16,0},{1,17},{17,1},{2,18},{18,2},{3,19},{19,3},{4,20},{20... | collective-permute-start | bytes 1769480 | tf_op jit(solution)/shard_map/ppermute | solution.py:56
  264.8 15.7 %copy-start.2 = (bf16[3,16,48,768]{3,2,1,0:T(8,128)(2,1)S(1)}, bf16[3,16,48,768]{3,2,1,0:T(8,128)(2,1)}, u32[]{:S(2)}) copy-start(bf16[3,16,48,768]{3,2,1,0:T(8,128)(2,1)} %copy-done.1) | copy-start | bytes 10616836
  326.5 20.5 %collective-permute-start.6 = (bf16[8,208,768]{2,1,0:T(8,128)(2,1)}, bf16[8,208,768]{2,1,0:T(8,128)(2,1)}, u32[]{:S(2)}, u32[]{:S(2)}) collective-permute-start(bf16[8,208,768]{2,1,0:T(8,128)(2,1)} %dynamic-slice_bitcast_fusion), channel_id=1, source_target_pairs={{0,1},{1,0},{2,3},{3,2},{4,5},{5,4},{6,7},{7,6},{8,9},{9,8},{10,11... | collective-permute-start | bytes 7667720 | tf_op jit(solution)/shard_map/ppermute | solution.py:45
  326.7 15.8 %collective-permute-start.8 = (bf16[8,96,384]{2,1,0:T(8,128)(2,1)}, bf16[8,96,384]{2,1,0:T(8,128)(2,1)S(1)}, u32[]{:S(2)}, u32[]{:S(2)}) collective-permute-start(bf16[8,96,384]{2,1,0:T(8,128)(2,1)} %all-to-all-done.1), channel_id=1, source_target_pairs={{0,16},{16,0},{1,17},{17,1},{2,18},{18,2},{3,19},{19,3},{4,20},{20... | collective-permute-start | bytes 1769480 | tf_op jit(solution)/shard_map/ppermute | solution.py:56
  330.5 14.2 %collective-permute-start.11 = (bf16[192,768]{1,0:T(8,128)(2,1)}, bf16[192,768]{1,0:T(8,128)(2,1)}, u32[]{:S(2)}, u32[]{:S(2)}) collective-permute-start(bf16[192,768]{1,0:T(8,128)(2,1)} %fusion.31), channel_id=1, source_target_pairs={{0,1},{1,0},{2,3},{3,2},{4,5},{5,4},{6,7},{7,6},{8,9},{9,8},{10,11... | collective-permute-start | bytes 884744 | tf_op jit(solution)/shard_map/ppermute | solution.py:45
  344.7 2.2 collective-permute-start.9
  390.1 8.4 %collective-permute-start.7 = (bf16[208,768]{1,0:T(8,128)(2,1)S(1)}, bf16[208,768]{1,0:T(8,128)(2,1)S(1)}, u32[]{:S(2)}, u32[]{:S(2)}) collective-permute-start(bf16[208,768]{1,0:T(8,128)(2,1)S(1)} %shard_map.190), channel_id=1, source_target_pairs={{0,16},{16,0},{1,17},{17,1},{2,18},{18,2},{3,19},{19,3},{4,20},{20... | collective-permute-start | bytes 958472 | tf_op jit(solution)/shard_map/ppermute | solution.py:56
  (58 other events, 209.1 us)
Sparse Core Ops, SparseCore 0:
  64.1 75.4 all-gather.1

commit v3 on v2

--- a/solution.py
+++ b/solution.py
@@ -20,25 +20,6 @@
 
 def gelu_tanh(values):
     return jax.nn.gelu(values, approximate=True)
-
-
-def offsets_to_pairs(per_offset, length):
-    heads = per_offset.shape[0]
-    reverse = per_offset[:, ::-1]
-    repeated = jnp.broadcast_to(reverse[:, None, :], (heads, length, 2 * length - 1))
-    repeated = repeated.reshape(heads, length * (2 * length - 1))
-    repeated = jnp.pad(repeated, ((0, 0), (0, length)))
-    skewed = repeated.reshape(heads, length, 2 * length)[:, :, :length]
-    return skewed[:, :, ::-1]
-
-
-def pairs_to_offsets(grid, length):
-    heads = grid.shape[0]
-    flipped = grid[:, :, ::-1]
-    padded = jnp.pad(flipped, ((0, 0), (0, 0), (0, length)))
-    flat = padded.reshape(heads, 2 * length * length)[:, : length * (2 * length - 1)]
-    skewed = flat.reshape(heads, length, 2 * length - 1)
-    return jnp.sum(skewed, axis=1)[:, ::-1]
 
 
 def swap(array, size):
@@ -268,6 +249,94 @@
     )(partial)
 
 
+def attend_kernel(heads, head_size, p_ref, bias_ref, down_ref, across_ref, c_ref, probs_ref):
+    length = p_ref.shape[1]
+    allowed = down_ref[...] == across_ref[...]
+    parts = []
+    for h in range(heads):
+        at = slice(h * head_size, (h + 1) * head_size)
+        raw = lax.dot_general(
+            p_ref[0, :, at],
+            p_ref[1, :, at],
+            (((1,), (1,)), ((), ())),
+            preferred_element_type=jnp.float32,
+        )
+        spread = jnp.broadcast_to(bias_ref[h : h + 1, :], (length, 2 * length))
+        skewed = pltpu.roll(spread, length + 1, 1, stride=1, stride_axis=0)
+        scores = jnp.where(allowed, raw * 0.125 + skewed[:, :length], -1e30)
+        expo = jnp.exp(scores - jnp.max(scores, axis=1, keepdims=True))
+        probs = expo / jnp.sum(expo, axis=1, keepdims=True)
+        probs_ref[h] = probs
+        parts.append(
+            jnp.dot(
+                probs.astype(jnp.bfloat16), p_ref[2, :, at], preferred_element_type=jnp.float32
+            )
+        )
+    c_ref[...] = jnp.concatenate(parts, axis=1).astype(c_ref.dtype)
+
+
+def attend(projected, offset_bias, segment, heads):
+    length, width = projected.shape[1:]
+    return pl.pallas_call(
+        functools.partial(attend_kernel, heads, width // heads),
+        out_shape=(
+            jax.ShapeDtypeStruct((length, width), jnp.bfloat16),
+            jax.ShapeDtypeStruct((heads, length, length), jnp.float32),
+        ),
+        compiler_params=pltpu.CompilerParams(vmem_limit_bytes=32 << 20),
+    )(projected, offset_bias, segment[:, None], segment[None, :])
+
+
+def attend_back_kernel(heads, head_size, p_ref, probs_ref, g_ref, o_ref, diag_ref):
+    length = p_ref.shape[1]
+    row = lax.broadcasted_iota(jnp.int32, (length, length), 0)
+    col = lax.broadcasted_iota(jnp.int32, (length, length), 1)
+    mirror = jnp.where(row + col == length - 1, 1.0, 0.0).astype(jnp.bfloat16)
+    blank = jnp.zeros((length, length), jnp.float32)
+    down = (((0,), (0,)), ((), ()))
+    parts = [[], [], []]
+    for h in range(heads):
+        at = slice(h * head_size, (h + 1) * head_size)
+        grad = g_ref[:, at]
+        probs = probs_ref[h]
+        prob_grad = lax.dot_general(
+            grad, p_ref[2, :, at], (((1,), (1,)), ((), ())), preferred_element_type=jnp.float32
+        )
+        total = jnp.sum(probs * prob_grad, axis=1, keepdims=True)
+        low = (probs * (prob_grad - total)).astype(jnp.bfloat16)
+        flipped = jnp.dot(low, mirror, preferred_element_type=jnp.float32)
+        skewed = pltpu.roll(
+            jnp.concatenate([flipped, blank], axis=1), 0, 1, stride=1, stride_axis=0
+        )
+        diag_ref[h : h + 1, :] = jnp.sum(skewed, axis=0, keepdims=True)
+        parts[0].append(
+            jnp.dot(low, p_ref[1, :, at], preferred_element_type=jnp.float32) * 0.125
+        )
+        parts[1].append(
+            lax.dot_general(low, p_ref[0, :, at], down, preferred_element_type=jnp.float32) * 0.125
+        )
+        parts[2].append(
+            lax.dot_general(
+                probs.astype(jnp.bfloat16), grad, down, preferred_element_type=jnp.float32
+            )
+        )
+    for k in range(3):
+        o_ref[k] = jnp.concatenate(parts[k], axis=1).astype(o_ref.dtype)
+
+
+def attend_back(projected, probs, context_grad):
+    heads, length = probs.shape[:2]
+    width = context_grad.shape[1]
+    return pl.pallas_call(
+        functools.partial(attend_back_kernel, heads, width // heads),
+        out_shape=(
+            jax.ShapeDtypeStruct((3, length, width), jnp.bfloat16),
+            jax.ShapeDtypeStruct((heads, 2 * length), jnp.float32),
+        ),
+        compiler_params=pltpu.CompilerParams(vmem_limit_bytes=32 << 20),
+    )(projected, probs, context_grad)
+
+
 def shards(
     size,
     reps,
@@ -288,7 +357,6 @@
     low = jnp.bfloat16
     length, width = tokens.shape
     heads = rel_table.shape[1]
-    head_size = width // heads
     experts = expert_in.shape[0]
     capacity = CAP
     bucket_count = BUCKETS
@@ -364,29 +432,16 @@
     projected = jnp.einsum(
         "td,kde->kte", normed, full_in, preferred_element_type=jnp.float32
     ).astype(low)
-    query = projected[0].reshape(length, heads, head_size)
-    keys = projected[1].reshape(length, heads, head_size)
-    values = projected[2].reshape(length, heads, head_size)
     offset_onehot = (
-        bucket_ids[:, None] == jnp.arange(bucket_count, dtype=jnp.int32)[None, :]
+        jnp.pad(bucket_ids, (0, 1), constant_values=-1)[:, None] == jnp.arange(bucket_count, dtype=jnp.int32)[None, :]
     ).astype(jnp.float32)
     offset_bias = jnp.einsum(
         "ob,bh->ho", offset_onehot, full_table.astype(jnp.float32), precision=highest
     )
-    bias = offsets_to_pairs(offset_bias, length)
     seqs = jnp.arange(lengths.shape[1], dtype=jnp.int32)
     ends = jnp.sum(jnp.where(seqs[None, :] <= seqs[:, None], lengths[0][None, :], 0), axis=1)
     segment = jnp.sum((places[:, None] >= ends[None, :]).astype(jnp.int32), axis=1)
-    allowed = segment[:, None] == segment[None, :]
-    raw = jnp.einsum("qhc,khc->hqk", query, keys, preferred_element_type=jnp.float32) * 0.125
-    scores = jnp.where(allowed[None], raw + bias, -1e30)
-    peak = jnp.max(scores, axis=-1, keepdims=True)
-    expo = jnp.exp(scores - peak)
-    totals = jnp.sum(expo, axis=-1, keepdims=True)
-    probs = expo / totals
-    probs_low = probs.astype(low)
-    context = jnp.einsum("hqk,khc->qhc", probs_low, values, preferred_element_type=jnp.float32)
-    context = context.astype(low).reshape(length, width)
+    context, probs = attend(projected, offset_bias, segment, heads)
     hidden = inputs + jnp.dot(context, full_out, preferred_element_type=jnp.float32)
     normed_ffn = rms_norm(hidden, gain_ffn).astype(low)
     logits = jnp.dot(normed_ffn, full_router, preferred_element_type=jnp.float32)
@@ -452,30 +507,12 @@
     attn_grad = hidden_grad.astype(low)
     attn_out_grad = jnp.einsum("td,te->de", context, attn_grad, preferred_element_type=jnp.float32)
     context_grad = jnp.einsum("te,de->td", attn_grad, full_out, preferred_element_type=jnp.float32)
-    context_grad = context_grad.astype(low).reshape(length, heads, head_size)
-    prob_grad_attn = jnp.einsum(
-        "qhc,khc->hqk", context_grad, values, preferred_element_type=jnp.float32
-    )
-    value_grad = jnp.einsum(
-        "hqk,qhc->khc", probs_low, context_grad, preferred_element_type=jnp.float32
-    )
-    score_grad = probs * (prob_grad_attn - jnp.sum(probs * prob_grad_attn, axis=-1, keepdims=True))
-    offset_grad = pairs_to_offsets(score_grad, length)
-    table_grad = jnp.einsum("ho,ob->bh", offset_grad, offset_onehot, precision=highest)
-    score_low = score_grad.astype(low)
-    query_grad = (
-        jnp.einsum("hqk,khc->qhc", score_low, keys, preferred_element_type=jnp.float32) * 0.125
-    )
-    key_grad = (
-        jnp.einsum("hqk,qhc->khc", score_low, query, preferred_element_type=jnp.float32) * 0.125
-    )
-    projected_grad = jnp.stack(
-        [
-            query_grad.reshape(length, width),
-            key_grad.reshape(length, width),
-            value_grad.reshape(length, width),
-        ]
-    ).astype(low)
+    context_grad = context_grad.astype(low)
+    projected_grad, diagonal = attend_back(projected, probs, context_grad)
+    offset_grad = diagonal[:, : 2 * length - 1][:, ::-1]
+    table_grad = jnp.einsum(
+        "ho,ob->bh", offset_grad, offset_onehot[: 2 * length - 1], precision=highest
+    )
     attn_in_grad = jnp.einsum(
         "td,kte->kde", normed, projected_grad, preferred_element_type=jnp.float32
     )
@@ -488,19 +525,26 @@
     gains_grad = jnp.stack([gain_attn_grad, gain_ffn_grad])
 
     def spread(values):
-        flat = values.astype(low).reshape(size, 1, -1)
+        flat = values.reshape(size, 1, -1)
         return jnp.pad(flat, ((0, 0), (0, 0), (0, width - flat.shape[2])))
 
-    grads = jnp.concatenate(
+    small = jnp.concatenate(
         [
-            jnp.transpose(attn_in_grad.astype(low).reshape(3, size, rows, width), (1, 0, 2, 3)).reshape(
-                size, 3 * rows, width
-            ),
-            attn_out_grad.astype(low).reshape(size, rows, width),
             spread(jnp.transpose(gains_grad.reshape(2, size, rows), (1, 0, 2))),
             spread(router_grad),
             spread(table_grad),
-            jnp.zeros((size, extra, width), low),
+            jnp.zeros((size, extra, width), jnp.float32),
+        ],
+        axis=1,
+    ).astype(low)
+    attn_in_grad = attn_in_grad.astype(low).reshape(3, size, rows, width)
+    grads = jnp.concatenate(
+        [
+            attn_in_grad[0],
+            attn_in_grad[1],
+            attn_in_grad[2],
+            attn_out_grad.astype(low).reshape(size, rows, width),
+            small,
         ],
         axis=1,
     ).reshape(chips, 2, depth, width)

time: 411 us -> 388 us (0.944)
  local copies, waits for them, and re-layouts: 95.9 us -> 74.1 us
  Pallas kernels: 187 us -> 196 us
  matrix products: 39.1 us -> 30.5 us
    unnamed x145 -> x98, local copies, waits for them, and re-layouts: 16.9 us -> 6.22 us
    pallas_call x0 -> x2, Pallas kernels: none -> 8.94 us  [the longest x1 4.64 us: attend_back(): pl.pallas_call(functools.partial(attend_back_kernel, heads, width // head...]
    reshape x6 -> x3, local copies, waits for them, and re-layouts: 7.45 us -> 0.38 us  [spread(): flat = values.reshape(size, 1, -1)]
    dot_general x7 -> x1, matrix products: 5.73 us -> 0.2 us  [shards(): jnp.einsum('ho,ob->bh', offset_grad, offset_onehot[:2 * length - 1], prec...]
    another operation x3 -> x2, local copies, waits for them, and re-layouts: 5.25 us -> 0.28 us  [shards(): jnp.stack([query_grad.reshape(length, width), key_grad.reshape(length, wi...]
    rev x2 -> x0, local copies, waits for them, and re-layouts: 4.16 us -> none  [the longest x1 3.86 us: pairs_to_offsets(): flipped = grid[:, :, ::-1]]
    concatenate x9 -> x11, local copies, waits for them, and re-layouts: 31.4 us -> 33.2 us  [the longest x5 32.4 us: shards(): jnp.concatenate([attn_in_grad[0], attn_in_grad[1], attn_in_grad[2], attn_...]
  transfers between devices with their start and end apart: 15 -> 15, of which waited for: 4 -> 4; matrix products, arithmetic and copies ran while one was open for 33% -> 27% of each run, Pallas kernels for 36% -> 41%
where the time goes in v3:
time: 388 us; the launch traced here: 385 us
  Pallas kernels  196 us (51%)
  local copies, waits for them, and re-layouts  74.1 us (19%)
  matrix products  30.5 us (8%)
  other arithmetic  26.2 us (7%)
  starting transfers between devices  23.9 us (6%)
  waiting for transfers between devices  19.7 us (5%)
  between operations  14.9 us (4%)
    pallas_call x2, Pallas kernels, scatter_chips(): pl.pallas_call(functools.partial(scatter_kernel, size), out_shape=jax.Sha...  97.1 us
    pallas_call x2, Pallas kernels, gather_chips(): pl.pallas_call(functools.partial(gather_kernel, size), out_shape=jax.Shap...  90 us
    concatenate x5, local copies, waits for them, and re-layouts, shards(): jnp.concatenate([attn_in_grad[0], attn_in_grad[1], attn_in_grad[2], attn_...  32.4 us
    ppermute x3, waiting for transfers between devices, rep_sum(): other = lax.ppermute(array, 'rep', [(0, 1), (1, 0)])  18.7 us
    all_to_all x1, starting transfers between devices, shards(): lax.all_to_all(in_rows, 'shard', 0, 0, axis_index_groups=groups, tiled=True)  10.1 us
    all_to_all x1, starting transfers between devices, shards(): lax.all_to_all(in_grad.astype(low).reshape(chips, 2 * rows, strip), 'shar...  9.4 us
  transfers between devices with their start and end apart: 15, of which 4 were waited for; matrix products, arithmetic and copies ran while one was open for 27% of the time, Pallas kernels for 41%

profile of v3, /device:TPU:0, one launch (start us, length us, event | category | flops | bytes accessed | tf_op | source)
XLA Modules:
  0.0 385.4 jit_solution(10492342199056981618)
XLA Ops:
  15.5 43.2 %shard_map.187 = bf16[8,208,768]{2,1,0:T(8,128)(2,1)S(1)} custom-call(bf16[208,768]{1,0:T(8,128)(2,1)S(1)} %pad.36.x_ref), custom_call_target="tpu_custom_call" | custom-call | tf_op jit(solution)/shard_map/pallas_call | solution.py:143
  66.8 10.1 %all-to-all-start = ((bf16[8,96,384]{2,1,0:T(8,128)(2,1)}), bf16[8,96,384]{2,1,0:T(8,128)(2,1)}, u32[]{:S(2)}, u32[]{:S(2)}) async-start(bf16[8,96,384]{2,1,0:T(8,128)(2,1)} %copy.96), calls=%async_computation | async-start | bytes 1179648 | tf_op jit(solution)/shard_map/all_to_all | solution.py:420
  81.4 2.6 copy.91
  86.5 2.4 slice.93
  88.9 2.2 slice.91
  96.1 4.3 %shard_map.188 = (bf16[128,768]{1,0:T(8,128)(2,1)S(1)}, f32[12,128,128]{2,1,0:T(8,128)S(1)}) custom-call(bf16[3,128,768]{2,1,0:T(8,128)(2,1)S(1)} %fusion.8.p_ref, f32[12,256]{1,0:T(8,128)S(1)} %fusion.36.bias_ref, s32[128,1]{1,0:T(8,128)S(1)} %copy-done.1, s32[1,128]{1,0:T(1,128)S(1)} %bitcast.119), custom_call_target="tpu_custom_call" | custom-call | tf_op jit(solution)/shard_map/pallas_call | solution.py:280
  102.9 46.8 %shard_map.189 = bf16[8,160,768]{2,1,0:T(8,128)(2,1)S(1)} custom-call(bf16[160,768]{1,0:T(8,128)(2,1)S(1)} %pad_maximum_fusion.8.x_ref), custom_call_target="tpu_custom_call" | custom-call | tf_op jit(solution)/shard_map/pallas_call | solution.py:143
  151.0 2.3 fusion.58
  154.6 2.7 convolution_convert_fusion.1
  157.3 4.6 %fusion.7 = bf16[1280,384]{1,0:T(8,128)(2,1)S(1)} fusion(f32[1280,384]{1,0:T(8,128)} %copy-done.45, bf16[1280,768]{1,0:T(8,128)(2,1)} %all-gather.2.cloned.1.call-done, f32[1280]{0:T(1024)} %divide_reduce_fusion, bf16[192,768]{1,0:T(8,128)(2,1)} %get-tuple-element.87, bf16[192,768]{1,0:T(8,128)(2,1)} %get-tuple-element.86), kind=kOutput, calls=%fused_computation.19 | convolution fusion | flops 768933888 | bytes 5510144 | tf_op jit(solution)/shard_map/cd,fd->cf/dot_general | solution.py:463
  163.9 3.7 convolution_convert_fusion
  167.7 9.4 %all-to-all-start.1 = ((bf16[8,96,384]{2,1,0:T(8,128)(2,1)}), bf16[8,96,384]{2,1,0:T(8,128)(2,1)}, u32[]{:S(2)}, u32[]{:S(2)}) async-start(bf16[8,96,384]{2,1,0:T(8,128)(2,1)} %bitcast.135), calls=%async_computation.1 | async-start | bytes 1179648 | tf_op jit(solution)/shard_map/all_to_all | solution.py:474
  177.1 3.7 pad_maximum_fusion.1
  180.7 6.3 %copy.97 = bf16[1280,1536]{1,0:T(8,128)(2,1)} copy(bf16[1280,1536]{0,1:T(8,128)(2,1)} %pad_maximum_fusion.1) | data formatting | bytes 7864320 | tf_op jit(solution)/shard_map/concatenate | solution.py:466
  189.1 57.3 %shard_map.190 = bf16[160,1536]{1,0:T(8,128)(2,1)S(1)} custom-call(bf16[8,160,1536]{2,1,0:T(8,128)(2,1)S(1)} %bitcast.114), custom_call_target="tpu_custom_call" | custom-call | tf_op jit(solution)/shard_map/pallas_call | solution.py:231
  246.5 2.2 convolution_convert_fusion.4
  255.8 4.6 %shard_map.191 = (bf16[3,128,768]{2,1,0:T(8,128)(2,1)S(1)}, f32[12,256]{1,0:T(8,128)S(1)}) custom-call(bf16[3,128,768]{2,1,0:T(8,128)(2,1)S(1)} %fusion.8.p_ref, f32[12,128,128]{2,1,0:T(8,128)S(1)} %get-tuple-element.14.probs_ref, bf16[128,768]{1,0:T(8,128)(2,1)S(1)} %convolution_convert_fusion.8.g_ref), custom_call_target="tpu_custom_call" | custom-call | tf_op jit(solution)/shard_map/pallas_call | solution.py:330
  260.5 4.1 %fusion.18 = (bf16[768]{0:T(1024)(128)(2,1)S(1)}, f32[128]{0:T(128)S(1)}, f32[128,768]{1,0:T(8,128)}) fusion(bf16[128,768]{1,0:T(8,128)(2,1)S(1)} %copy-done.7, f32[128]{0:T(128)S(1)} %copy-done.28, f32[768]{0:T(1024)S(1)} %reshape.228, bf16[3,128,768]{2,1,0:T(8,128)(2,1)S(1)} %get-tuple-element.15, bf16[3,768,768]{2,1,0:T(8,128)(2,1)} %bitcast.121), kind=kOutput, calls=%fused_computation.64 | convolution fusion | flops 453672064 | bytes 4724224 | tf_op jit(solution)/shard_map/kte,kde->td/dot_general | solution.py:519
  270.7 28.8 %concatenate.65 = bf16[8,2,208,768]{3,2,0,1:T(8,128)(2,1)} concatenate(bf16[8,2,48,768]{3,2,0,1:T(8,128)(2,1)} %copy.102, bf16[8,2,48,768]{3,2,0,1:T(8,128)(2,1)} %copy.103, bf16[8,2,48,768]{3,2,0,1:T(8,128)(2,1)S(1)} %copy.104, bf16[8,2,48,768]{3,2,0,1:T(8,128)(2,1)S(1)} %copy.105, bf16[8,2,1,768]{3,2,0,1:T(2,128)(2,1)S(1)} %copy.106, bf16[8,2,1,768]{3,2,0,1:T(2,128)(2,1)S(1)} %copy-done.23, ...), dimensions={2} | concatenate | bytes 10223616 | tf_op jit(solution)/shard_map/concatenate | solution.py:541
  299.5 3.5 dynamic-slice_bitcast_fusion
  307.0 12.0 %collective-permute-done.8 = bf16[8,96,384]{2,1,0:T(8,128)(2,1)S(1)} collective-permute-done((bf16[8,96,384]{2,1,0:T(8,128)(2,1)}, bf16[8,96,384]{2,1,0:T(8,128)(2,1)S(1)}, u32[]{:S(2)}, u32[]{:S(2)}) %collective-permute-start.8) | collective-permute-done | bytes 589856 | tf_op jit(solution)/shard_map/ppermute | solution.py:37
  323.5 3.1 fusion.p_ref
  326.7 39.9 %shard_map.192 = bf16[208,768]{1,0:T(8,128)(2,1)S(1)} custom-call(bf16[8,208,768]{2,1,0:T(8,128)(2,1)S(1)} %fusion.p_ref), custom_call_target="tpu_custom_call" | custom-call | tf_op jit(solution)/shard_map/pallas_call | solution.py:231
  368.3 6.7 %collective-permute-done.7 = bf16[208,768]{1,0:T(8,128)(2,1)S(1)} collective-permute-done((bf16[208,768]{1,0:T(8,128)(2,1)S(1)}, bf16[208,768]{1,0:T(8,128)(2,1)S(1)}, u32[]{:S(2)}, u32[]{:S(2)}) %collective-permute-start.7) | collective-permute-done | bytes 319520 | tf_op jit(solution)/shard_map/ppermute | solution.py:37
  (236 shorter events, 64.1 us)
Async XLA Ops:
  7.2 150.1 %all-gather.2.cloned.1.call-start = ((), (), s32[]{:S(2)}) async-start(), calls=%async_computation.2 | async-start | bytes 2211840 | tf_op jit(solution)/shard_map/all_gather | solution.py:385
  10.6 51.9 %collective-permute-start.4 = (bf16[80,768]{1,0:T(8,128)(2,1)}, bf16[80,768]{1,0:T(8,128)(2,1)}, u32[]{:S(2)}, u32[]{:S(2)}) collective-permute-start(bf16[80,768]{1,0:T(8,128)(2,1)} %get-tuple-element.95), channel_id=1, source_target_pairs={{0,1},{1,0},{2,3},{3,2},{4,5},{5,4},{6,7},{7,6},{8,9},{9,8},{10,11... | collective-permute-start | bytes 368648 | tf_op jit(solution)/shard_map/ppermute | solution.py:26
  13.5 45.3 %copy-start.20 = (bf16[2,192,768]{2,1,0:T(8,128)(2,1)S(1)}, bf16[2,192,768]{2,1,0:T(8,128)(2,1)}, u32[]{:S(2)}) copy-start(bf16[2,192,768]{2,1,0:T(8,128)(2,1)} %param.23) | copy-start | bytes 1769476
  15.5 44.6 %copy-start.19 = (bf16[2,48,3072]{2,1,0:T(8,128)(2,1)S(1)}, bf16[2,48,3072]{2,1,0:T(8,128)(2,1)}, u32[]{:S(2)}) copy-start(bf16[2,48,3072]{2,1,0:T(8,128)(2,1)} %param.22) | copy-start | bytes 1769476
  15.5 44.7 %copy-start.44 = (s32[1,3]{1,0:T(1,128)S(1)}, s32[1,3]{1,0:T(1,128)}, u32[]{:S(2)}) copy-start(s32[1,3]{1,0:T(1,128)} %param.14) | copy-start | bytes 40
  15.5 45.6 %copy-start.38 = (s32[255]{0:T(256)S(1)}, s32[255]{0:T(256)}, u32[]{:S(2)}) copy-start(s32[255]{0:T(256)} %param.16) | copy-start | bytes 3064
  15.5 45.6 %copy-start.5 = (bf16[128,768]{1,0:T(8,128)(2,1)S(1)}, bf16[128,768]{1,0:T(8,128)(2,1)}, u32[]{:S(2)}) copy-start(bf16[128,768]{1,0:T(8,128)(2,1)} %param.12) | copy-start | bytes 589828
  58.7 20.1 %collective-permute-start = (bf16[8,208,768]{2,1,0:T(8,128)(2,1)S(1)}, bf16[8,208,768]{2,1,0:T(8,128)(2,1)}, u32[]{:S(2)}, u32[]{:S(2)}) collective-permute-start(bf16[8,208,768]{2,1,0:T(8,128)(2,1)S(1)} %shard_map.187), channel_id=1, source_target_pairs={{0,1},{1,0},{2,3},{3,2},{4,5},{5,4},{6,7},{7,6},{8,9},{9,8},{10,11... | collective-permute-start | bytes 7667720 | tf_op jit(solution)/shard_map/ppermute | solution.py:26
  59.6 17.3 %collective-permute-start.3 = (bf16[192,768]{1,0:T(8,128)(2,1)}, bf16[192,768]{1,0:T(8,128)(2,1)}, u32[]{:S(2)}, u32[]{:S(2)}) collective-permute-start(bf16[192,768]{1,0:T(8,128)(2,1)} %dynamic-slice_bitcast_fusion.1), channel_id=1, source_target_pairs={{0,1},{1,0},{2,3},{3,2},{4,5},{5,4},{6,7},{7,6},{8,9},{9,8},{10,11... | collective-permute-start | bytes 884744 | tf_op jit(solution)/shard_map/ppermute | solution.py:26
  60.1 4.5 %collective-permute-start.2 = (bf16[48,3072]{1,0:T(8,128)(2,1)S(1)}, bf16[48,3072]{1,0:T(8,128)(2,1)}, u32[]{:S(2)}, u32[]{:S(2)}) collective-permute-start(bf16[48,3072]{1,0:T(8,128)(2,1)S(1)} %dynamic-slice_bitcast_fusion.2), channel_id=1, source_target_pairs={{0,1},{1,0},{2,3},{3,2},{4,5},{5,4},{6,7},{7,6},{8,9},{9,8},{10,11... | collective-permute-start | bytes 884744 | tf_op jit(solution)/shard_map/ppermute | solution.py:26
  66.8 84.3 %all-to-all-start = ((bf16[8,96,384]{2,1,0:T(8,128)(2,1)}), bf16[8,96,384]{2,1,0:T(8,128)(2,1)}, u32[]{:S(2)}, u32[]{:S(2)}) async-start(bf16[8,96,384]{2,1,0:T(8,128)(2,1)} %copy.96), calls=%async_computation | async-start | bytes 1179648 | tf_op jit(solution)/shard_map/all_to_all | solution.py:420
  101.5 1.3 collective-permute-start.1
  163.9 13.1 %copy-start.16 = (bf16[1280,768]{0,1:T(8,128)(2,1)S(1)}, bf16[1280,768]{0,1:T(8,128)(2,1)}, u32[]{:S(2)}) copy-start(bf16[1280,768]{0,1:T(8,128)(2,1)} %convolution_convert_fusion.1) | copy-start | bytes 5898244
  167.7 135.5 %all-to-all-start.1 = ((bf16[8,96,384]{2,1,0:T(8,128)(2,1)}), bf16[8,96,384]{2,1,0:T(8,128)(2,1)}, u32[]{:S(2)}, u32[]{:S(2)}) async-start(bf16[8,96,384]{2,1,0:T(8,128)(2,1)} %bitcast.135), calls=%async_computation.1 | async-start | bytes 1179648 | tf_op jit(solution)/shard_map/all_to_all | solution.py:474
  189.1 57.4 %copy-start.26 = (f32[1280]{0:T(1024)S(1)}, f32[1280]{0:T(1024)}, u32[]{:S(2)}) copy-start(f32[1280]{0:T(1024)} %divide_reduce_fusion) | copy-start | bytes 15364
  189.1 57.4 %copy-start.43 = (bf16[1280,768]{1,0:T(8,128)(2,1)S(1)}, bf16[1280,768]{1,0:T(8,128)(2,1)}, u32[]{:S(2)}) copy-start(bf16[1280,768]{1,0:T(8,128)(2,1)} %all-gather.2.cloned.1.call-done) | copy-start | bytes 5898244
  189.1 57.4 %copy-start.46 = (f32[1280,384]{1,0:T(8,128)S(1)}, f32[1280,384]{1,0:T(8,128)}, u32[]{:S(2)}) copy-start(f32[1280,384]{1,0:T(8,128)} %copy-done.45) | copy-start | bytes 5898244
  246.4 3.9 %collective-permute-start.5 = (bf16[80,1536]{1,0:T(8,128)(2,1)S(1)}, bf16[80,1536]{1,0:T(8,128)(2,1)S(1)}, u32[]{:S(2)}, u32[]{:S(2)}) collective-permute-start(bf16[80,1536]{1,0:T(8,128)(2,1)S(1)} %slice.76), channel_id=1, source_target_pairs={{0,1},{1,0},{2,3},{3,2},{4,5},{5,4},{6,7},{7,6},{8,9},{9,8},{10,11... | collective-permute-start | bytes 737288 | tf_op jit(solution)/shard_map/ppermute | solution.py:26
  248.8 56.1 %collective-permute-start.10 = (bf16[384,768]{1,0:T(8,128)(2,1)}, bf16[384,768]{1,0:T(8,128)(2,1)}, u32[]{:S(2)}, u32[]{:S(2)}) collective-permute-start(bf16[384,768]{1,0:T(8,128)(2,1)} %convolution_convert_fusion.4), channel_id=1, source_target_pairs={{0,16},{16,0},{1,17},{17,1},{2,18},{18,2},{3,19},{19,3},{4,20},{20... | collective-permute-start | bytes 1769480 | tf_op jit(solution)/shard_map/ppermute | solution.py:37
  303.0 20.5 %collective-permute-start.6 = (bf16[8,208,768]{2,1,0:T(8,128)(2,1)}, bf16[8,208,768]{2,1,0:T(8,128)(2,1)}, u32[]{:S(2)}, u32[]{:S(2)}) collective-permute-start(bf16[8,208,768]{2,1,0:T(8,128)(2,1)} %dynamic-slice_bitcast_fusion), channel_id=1, source_target_pairs={{0,1},{1,0},{2,3},{3,2},{4,5},{5,4},{6,7},{7,6},{8,9},{9,8},{10,11... | collective-permute-start | bytes 7667720 | tf_op jit(solution)/shard_map/ppermute | solution.py:26
  303.2 15.8 %collective-permute-start.8 = (bf16[8,96,384]{2,1,0:T(8,128)(2,1)}, bf16[8,96,384]{2,1,0:T(8,128)(2,1)S(1)}, u32[]{:S(2)}, u32[]{:S(2)}) collective-permute-start(bf16[8,96,384]{2,1,0:T(8,128)(2,1)} %all-to-all-done.1), channel_id=1, source_target_pairs={{0,16},{16,0},{1,17},{17,1},{2,18},{18,2},{3,19},{19,3},{4,20},{20... | collective-permute-start | bytes 1769480 | tf_op jit(solution)/shard_map/ppermute | solution.py:37
  307.0 14.2 %collective-permute-start.11 = (bf16[192,768]{1,0:T(8,128)(2,1)}, bf16[192,768]{1,0:T(8,128)(2,1)}, u32[]{:S(2)}, u32[]{:S(2)}) collective-permute-start(bf16[192,768]{1,0:T(8,128)(2,1)} %fusion.24), channel_id=1, source_target_pairs={{0,1},{1,0},{2,3},{3,2},{4,5},{5,4},{6,7},{7,6},{8,9},{9,8},{10,11... | collective-permute-start | bytes 884744 | tf_op jit(solution)/shard_map/ppermute | solution.py:26
  321.2 2.2 collective-permute-start.9
  366.5 8.4 %collective-permute-start.7 = (bf16[208,768]{1,0:T(8,128)(2,1)S(1)}, bf16[208,768]{1,0:T(8,128)(2,1)S(1)}, u32[]{:S(2)}, u32[]{:S(2)}) collective-permute-start(bf16[208,768]{1,0:T(8,128)(2,1)S(1)} %shard_map.192), channel_id=1, source_target_pairs={{0,16},{16,0},{1,17},{17,1},{2,18},{18,2},{3,19},{19,3},{4,20},{20... | collective-permute-start | bytes 958472 | tf_op jit(solution)/shard_map/ppermute | solution.py:37
  (38 other events, 113.5 us)
Sparse Core Ops, SparseCore 0:
  64.3 75.8 all-gather.1
